TPU v7x, 32 devices: a whole 2x2x4 slice. The times are simulated.
32 devices in a mesh: img: 8 (over z, x), sp: 4 (over y, core).
Axes of the slice: x: 2, y: 2, z: 4, core: 2. Of those that a mesh axis runs over, the one named last changes fastest.
Arguments:
- student: bfloat16 [96, 8, 8, 1280], P('img', 'sp')
- dino_feats: bfloat16 [48, 4, 4, 1536], P('img', 'sp'), may hold values from -6 to 6
- sam_feats: bfloat16 [48, 16, 16, 1280], P('img', 'sp'), may hold values from -6 to 6
- dino_proj: bfloat16 [1280, 1536], P('sp'), may hold values from -0.15625 to 0.15625
- sam_proj: bfloat16 [1280, 1280], P('sp'), may hold values from -0.15625 to 0.15625
- dino_list: int32 [48], replicated, may hold values from 0 to 95, as said below
- sam_list: int32 [48], replicated, may hold values from 0 to 95, as said below
- dino_row_weight: float32 [8, 3], replicated, may hold values from 0.2 to 1
- dino_col_weight: float32 [8, 4], replicated, may hold values from 0.1 to 0.6
- sam_start: int32 [8], replicated, may hold values from -2 to 14, as said below
- sam_row_weight: float32 [8, 4], replicated, may hold values from 0.2 to 1
- sam_col_weight: float32 [8, 16], replicated, may hold values from 0.05 to 0.35
Outputs:
- student_grad: bfloat16 [96, 8, 8, 1280], P('img', 'sp')
Inputs may be any that keep to these rules, and one draw needn't show every extreme that they name: `dino_list`: entries are distinct student images; image i belongs to img index i // 12, and slot q lies on img index q // 6. One img index holds at most 2 slots of images of any one owner. Each owner has at most 12 images in the list, and some owner has exactly that many. `sam_list`: as for dino_list, drawn independently. sam_start[y] is 2 y - 2 + (y mod 2) or one more.
All inputs are finite; a program needn't handle non-finite values.
Results may differ from a plain program's by a relative error of at most 0.015.
Values may be sent and summed in bfloat16 or wider, within the bound.
No kernel may reach another device: no remote copies, remote signals or barrier semaphores. Data moves between devices by JAX's collectives and lax.ppermute only.
A program may use at most 64 MiB of HBM per device.

v0:
```python
import jax
import jax.numpy as jnp
from jax import lax
from jax.sharding import PartitionSpec as P

HIGHEST = lax.Precision.HIGHEST
EPSILON = 1e-06


def padded_2(x, sides, width):
    for axis, dim in sides:
        count, length = (lax.axis_size(axis), x.shape[dim])
        up = [(i, (i + 1) % count) for i in range(count - 1)]
        down = [(j, i) for i, j in up]
        last = lax.slice_in_dim(x, length - width, length, axis=dim)
        first = lax.slice_in_dim(x, 0, width, axis=dim)
        before = lax.ppermute(last, axis, up)
        after = lax.ppermute(first, axis, down)
        x = jnp.concatenate([before, x, after], axis=dim)
    return x


def route_tables(slot_images, peer_count, image_dev, rank_now):
    per_device = slot_images.shape[0] // peer_count
    capacity = (2 * per_device + peer_count - 1) // peer_count
    table = slot_images.reshape(peer_count, per_device)
    owner_of = table // image_dev
    local_of = table % image_dev
    earlier = jnp.arange(per_device)[:, None] > jnp.arange(per_device)[None, :]
    same_owner = owner_of[:, :, None] == owner_of[:, None, :]
    position = jnp.sum(jnp.where(same_owner & earlier[None], 1, 0), axis=2)
    buffer_index = owner_of * capacity + position
    own_index = lax.dynamic_index_in_dim(buffer_index, rank_now, 0, keepdims=False)
    buffer_rows = jnp.arange(peer_count * capacity)
    packer = jnp.where(buffer_rows[:, None] == own_index[None, :], 1.0, 0.0).astype(jnp.bfloat16)
    source_row = jnp.arange(peer_count)[:, None] * capacity + position
    is_mine = owner_of == rank_now
    local_hot = jnp.where(
        is_mine[:, :, None] & (local_of[:, :, None] == jnp.arange(image_dev)[None, None, :]),
        1.0,
        0.0,
    )
    column_hot = jnp.where(source_row[:, :, None] == buffer_rows[None, None, :], 1.0, 0.0)
    placer = jnp.einsum("rtk,rtc->kc", local_hot, column_hot).astype(jnp.bfloat16)
    taught = jnp.sum(placer.astype(jnp.float32), axis=1)
    return (packer, placer, taught)


def apply_rows(matrix, values):
    flattened = values.reshape(values.shape[0], -1)
    product = jnp.dot(matrix, flattened, preferred_element_type=jnp.float32).astype(jnp.bfloat16)
    return product.reshape((matrix.shape[0],) + values.shape[1:])


def resample_rows(row_local, col_weight, padded):
    across = jnp.einsum("xj,bkjc->bkxc", col_weight, padded.astype(jnp.float32), precision=HIGHEST)
    result = jnp.einsum("yk,bkxc->byxc", row_local, across, precision=HIGHEST)
    return result.astype(jnp.bfloat16)


def sam_local(sam_start, row_weight, sp_rank):
    start_here = lax.dynamic_slice_in_dim(sam_start, 2 * sp_rank, 2, 0)
    weight_here = lax.dynamic_slice_in_dim(row_weight, 2 * sp_rank, 2, 0)
    local_rows = jnp.arange(8)[None, :]
    matrix = jnp.zeros((2, 8), jnp.float32)
    for tap_index in range(row_weight.shape[1]):
        hit = local_rows == (start_here - 4 * sp_rank + 2 + tap_index)[:, None]
        matrix = matrix + jnp.where(hit, weight_here[:, tap_index : tap_index + 1], 0.0)
    return matrix


def cosine_back(student_rows, target, weight, mask_rows):
    predicted = jnp.dot(student_rows, weight, preferred_element_type=jnp.float32)
    target_wide = target.astype(jnp.float32)
    pred_norm = jnp.sqrt(jnp.sum(predicted * predicted, axis=-1, keepdims=True) + EPSILON)
    goal_norm = jnp.sqrt(jnp.sum(target_wide * target_wide, axis=-1, keepdims=True) + EPSILON)
    cosine = jnp.sum(predicted * target_wide, axis=-1, keepdims=True) / (pred_norm * goal_norm)
    feature_count = predicted.shape[-1]
    delta = feature_count * (
        cosine * predicted / (pred_norm * pred_norm) - target_wide / (pred_norm * goal_norm)
    )
    delta = (delta * mask_rows).astype(jnp.bfloat16)
    grad_rows = lax.dot_general(
        delta, weight, (((1,), (1,)), ((), ())), preferred_element_type=jnp.float32
    )
    return grad_rows.astype(jnp.bfloat16)


def smooth_back(student_rows, target, weight, mask_rows):
    predicted = jnp.dot(student_rows, weight, preferred_element_type=jnp.float32)
    delta = jnp.clip(predicted - target.astype(jnp.float32), -1.0, 1.0)
    delta = (delta * mask_rows).astype(jnp.bfloat16)
    grad_rows = lax.dot_general(
        delta, weight, (((1,), (1,)), ((), ())), preferred_element_type=jnp.float32
    )
    return grad_rows.astype(jnp.bfloat16)


def image_grads(loss_back, student_part, target, weight, taught):
    images, rows_dev, cols_dev, width = student_part.shape
    mask_rows = jnp.repeat(taught, rows_dev * cols_dev)[:, None]
    student_rows = student_part.reshape(images * rows_dev * cols_dev, width)
    grad_rows = loss_back(
        student_rows, target.reshape(student_rows.shape[0], -1), weight, mask_rows
    )
    return grad_rows.reshape(student_part.shape)


def owner_path(features, tables, row_local, col_weight, weight, student, loss_back, rim, carry_raw):
    packer, placer, taught = tables
    arrived = carry_raw(apply_rows(packer, features))
    padded = rim(apply_rows(placer, arrived))
    target = resample_rows(row_local, col_weight, padded)
    return image_grads(loss_back, student, target, weight, taught)


def shards(
    student,
    dino_feats,
    sam_feats,
    dino_proj,
    sam_proj,
    dino_list,
    sam_list,
    dino_row_weight,
    dino_col_weight,
    sam_start,
    sam_row_weight,
    sam_col_weight,
):
    dino_full, sam_full = (
        lax.all_gather(dino_proj, "sp", axis=0, tiled=True),
        lax.all_gather(sam_proj, "sp", axis=0, tiled=True),
    )
    peer_count = lax.axis_size("img")
    rank_now = lax.axis_index("img")
    sp_rank = lax.axis_index("sp")
    image_dev = student.shape[0]
    dino_tables = route_tables(dino_list, peer_count, image_dev, rank_now)
    sam_tables = route_tables(sam_list, peer_count, image_dev, rank_now)
    dino_rows_here = lax.dynamic_slice_in_dim(dino_row_weight, 2 * sp_rank, 2, 0)
    sam_rows_here = sam_local(sam_start, sam_row_weight, sp_rank)

    def dino_rim(values):
        return padded_2(values, (("sp", 1),), 1)

    def sam_rim(values):
        return padded_2(values, (("sp", 1),), 2)

    def dino_carry(values):
        return lax.all_to_all(values, "img", split_axis=0, concat_axis=0, tiled=True)

    dino_grad = owner_path(
        dino_feats,
        dino_tables,
        dino_rows_here,
        dino_col_weight,
        dino_full,
        student,
        cosine_back,
        dino_rim,
        dino_carry,
    )

    def sam_carry(values):
        return lax.all_to_all(values, "img", split_axis=0, concat_axis=0, tiled=True)

    sam_grad = owner_path(
        sam_feats,
        sam_tables,
        sam_rows_here,
        sam_col_weight,
        sam_full,
        student,
        smooth_back,
        sam_rim,
        sam_carry,
    )
    return (dino_grad.astype(jnp.float32) + sam_grad.astype(jnp.float32)).astype(jnp.bfloat16)


def solution(mesh):
    placed = (
        P("img", "sp", None, None),
        P("img", "sp", None, None),
        P("img", "sp", None, None),
        P("sp", None),
        P("sp", None),
        P(),
        P(),
        P(),
        P(),
        P(),
        P(),
        P(),
    )
    return jax.shard_map(
        shards, mesh=mesh, in_specs=placed, out_specs=P("img", "sp", None, None), check_vma=False
    )
```

profile of v0, /device:TPU:1, one launch (start us, length us, event | category | flops | bytes accessed | tf_op | source)
XLA Modules:
  0.0 140.4 jit_solution(2952310112423499936)
XLA Ops:
  6.5 0.7 all-gather.3.cloned.1.call-update
  7.3 0.7 broadcast_remainder_fusion.1
  8.1 0.7 broadcast_remainder_fusion
  9.3 0.7 sign_compare_fusion.1
  10.1 0.7 sign_compare_fusion
  11.2 0.9 copy.103
  12.8 0.8 reshape.254
  13.6 6.4 %all-to-all-start = ((bf16[16,1,4,1536]{3,2,1,0:T(4,128)(2,1)}), bf16[16,1,4,1536]{3,2,1,0:T(4,128)(2,1)S(1)}, u32[]{:S(2)}, u32[]{:S(2)}) async-start(bf16[16,1,4,1536]{3,2,1,0:T(4,128)(2,1)} %bitcast.2), calls=%async_computation | async-start | bytes 393216 | tf_op jit(solution)/shard_map/all_to_all | solution.py:151
  20.2 0.6 copy.105
  20.8 0.8 convolution_convert_fusion.1
  21.6 2.1 %copy.106 = bf16[2,8,64,1280]{3,2,1,0:T(8,128)(2,1)} copy(bf16[2,8,64,1280]{3,1,2,0:T(8,128)(2,1)S(1)} %bitcast.91) | data formatting | bytes 5242880
  23.7 3.0 %all-to-all-done = bf16[16,1,4,1536]{3,2,1,0:T(4,128)(2,1)S(1)} async-done(((bf16[16,1,4,1536]{3,2,1,0:T(4,128)(2,1)}), bf16[16,1,4,1536]{3,2,1,0:T(4,128)(2,1)S(1)}, u32[]{:S(2)}, u32[]{:S(2)}) %all-to-all-start) | async-done | bytes 196640 | tf_op jit(solution)/shard_map/all_to_all | solution.py:151
  26.7 4.3 %all-to-all-start.1 = ((bf16[16,4,16,1280]{3,2,1,0:T(8,128)(2,1)}), bf16[16,4,16,1280]{3,2,1,0:T(8,128)(2,1)S(1)}, u32[]{:S(2)}, u32[]{:S(2)}) async-start(bf16[16,4,16,1280]{3,2,1,0:T(8,128)(2,1)} %bitcast.43), calls=%async_computation.1 | async-start | bytes 5242880 | tf_op jit(solution)/shard_map/all_to_all | solution.py:166
  31.0 0.7 all-gather.5.cloned.1.call-update
  33.2 0.7 reshape.256
  33.9 4.8 %collective-permute-start = (bf16[12,1,4,1536]{3,2,1,0:T(4,128)(2,1)}, bf16[12,1,4,1536]{3,2,1,0:T(4,128)(2,1)}, u32[]{:S(2)}, u32[]{:S(2)}) collective-permute-start(bf16[12,1,4,1536]{3,2,1,0:T(4,128)(2,1)} %bitcast.3), channel_id=1, source_target_pairs={{0,1},{1,2},{2,3},{4,5},{5,6},{6,7},{8,9},{9,10},{10,11},{12,13},{... | collective-permute-start | bytes 442376 | tf_op jit(solution)/shard_map/ppermute | solution.py:17
  38.7 1.9 %collective-permute-start.1 = (bf16[12,1,4,1536]{3,2,1,0:T(4,128)(2,1)}, bf16[12,1,4,1536]{3,2,1,0:T(4,128)(2,1)}, u32[]{:S(2)}, u32[]{:S(2)}) collective-permute-start(bf16[12,1,4,1536]{3,2,1,0:T(4,128)(2,1)} %bitcast.3), channel_id=1, source_target_pairs={{1,0},{2,1},{3,2},{5,4},{6,5},{7,6},{9,8},{10,9},{11,10},{13,12},{... | collective-permute-start | bytes 442376 | tf_op jit(solution)/shard_map/ppermute | solution.py:18
  40.6 48.2 %all-to-all-done.1 = bf16[16,4,16,1280]{3,2,1,0:T(8,128)(2,1)S(1)} async-done(((bf16[16,4,16,1280]{3,2,1,0:T(8,128)(2,1)}), bf16[16,4,16,1280]{3,2,1,0:T(8,128)(2,1)S(1)}, u32[]{:S(2)}, u32[]{:S(2)}) %all-to-all-start.1) | async-done | bytes 2621472 | tf_op jit(solution)/shard_map/all_to_all | solution.py:166
  88.8 1.4 %copy.107 = bf16[2,8,64,1280]{3,1,2,0:T(8,128)(2,1)S(1)} copy(bf16[2,8,64,1280]{3,2,1,0:T(8,128)(2,1)S(1)} %bitcast.89) | data formatting | bytes 5242880
  90.3 0.8 convolution_convert_fusion
  91.8 1.1 fusion.110
  92.9 5.6 %collective-permute-start.2 = (bf16[12,2,16,1280]{3,2,1,0:T(8,128)(2,1)}, bf16[12,2,16,1280]{3,2,1,0:T(8,128)(2,1)}, u32[]{:S(2)}, u32[]{:S(2)}) collective-permute-start(bf16[12,2,16,1280]{3,2,1,0:T(8,128)(2,1)} %get-tuple-element.17), channel_id=1, source_target_pairs={{0,1},{1,2},{2,3},{4,5},{5,6},{6,7},{8,9},{9,10},{10,11},{12,13},{... | collective-permute-start | bytes 2949128 | tf_op jit(solution)/shard_map/ppermute | solution.py:17
  98.5 1.9 %collective-permute-start.3 = (bf16[12,2,16,1280]{3,2,1,0:T(8,128)(2,1)S(1)}, bf16[12,2,16,1280]{3,2,1,0:T(8,128)(2,1)}, u32[]{:S(2)}, u32[]{:S(2)}) collective-permute-start(bf16[12,2,16,1280]{3,2,1,0:T(8,128)(2,1)S(1)} %get-tuple-element.18), channel_id=1, source_target_pairs={{1,0},{2,1},{3,2},{5,4},{6,5},{7,6},{9,8},{10,9},{11,10},{13,12},{... | collective-permute-start | bytes 2949128 | tf_op jit(solution)/shard_map/ppermute | solution.py:18
  100.5 2.1 %convolution_bitcast_fusion = f32[12,3,8,1536]{3,2,1,0:T(8,128)S(1)} fusion(bf16[12,1,4,1536]{3,2,1,0:T(4,128)(2,1)} %collective-permute-done.1, bf16[12,1,4,1536]{3,2,1,0:T(4,128)(2,1)} %bitcast.3, bf16[12,1,4,1536]{3,2,1,0:T(4,128)(2,1)} %collective-permute-done, f32[8,4]{0,1:T(4,128)S(1)} %copy-done.5), kind=kOutput, calls=%fused_computation.13 | convolution fusion | flops 22560768 | bytes 2211968 | tf_op jit(solution)/shard_map/xj,bkjc->bkxc/dot_general | solution.py:56
  102.5 5.6 %multiply_reduce_fusion = (f32[12,8,2]{2,1,0:T(8,128)S(1)}, f32[12,8,1536,2]{2,3,1,0:T(2,128)S(1)}) fusion(f32[8,3]{0,1:T(4,128)S(1)} %copy-done.4, s32[]{:T(128)S(6)} %select_n.107, f32[12,3,8,1536]{3,2,1,0:T(8,128)S(1)} %convolution_bitcast_fusion), kind=kOutput, calls=%fused_computation.31 | convolution fusion | flops 11796288 | bytes 2949988 | tf_op jit(solution)/shard_map/yk,bkxc->byxc/dot_general | solution.py:57
  108.1 1.2 copy.86
  109.8 4.2 %collective-permute-done.3 = bf16[12,2,16,1280]{3,2,1,0:T(8,128)(2,1)} collective-permute-done((bf16[12,2,16,1280]{3,2,1,0:T(8,128)(2,1)S(1)}, bf16[12,2,16,1280]{3,2,1,0:T(8,128)(2,1)}, u32[]{:S(2)}, u32[]{:S(2)}) %collective-permute-start.3) | collective-permute-done | bytes 983072 | tf_op jit(solution)/shard_map/ppermute | solution.py:18
  114.0 3.4 %fusion.8 = f32[12,8,8,1280]{3,2,1,0:T(8,128)S(1)} fusion(bf16[12,2,16,1280]{3,2,1,0:T(8,128)(2,1)} %collective-permute-done.3, bf16[12,4,16,1280]{3,2,1,0:T(8,128)(2,1)S(1)} %bitcast.95, bf16[12,2,16,1280]{3,2,1,0:T(8,128)(2,1)} %collective-permute-done.2, f32[8,16]{1,0:T(8,128)S(1)} %copy-done.8), kind=kOutput, calls=%fused_computation.12 | convolution fusion | flops 192675840 | bytes 7864832 | tf_op jit(solution)/shard_map/xj,bkjc->bkxc/dot_general | solution.py:56
  117.5 4.4 %fusion.23 = f32[12,2,8,1280]{3,1,2,0:T(2,128)S(1)} fusion(f32[12,8,8,1280]{3,2,1,0:T(8,128)S(1)} %fusion.8, f32[2]{0:T(128)S(1)} %get-tuple-element.24, s32[2]{0:T(128)S(1)} %get-tuple-element.30, f32[2]{0:T(128)S(1)} %get-tuple-element.25, s32[2]{0:T(128)S(1)} %get-tuple-element.29, f32[2]{0:T(128)S(1)} %get-tuple-element.26, ...), kind=kOutput, calls=%fused_computation.24 | convolution fusion | flops 24084656 | bytes 4915264 | tf_op jit(solution)/shard_map/yk,bkxc->byxc/dot_general | solution.py:57
  122.0 3.4 %multiply_reduce_fusion.2 = (f32[192]{0:T(256)S(1)}, f32[192]{0:T(256)S(1)}, f32[192,1536]{1,0:T(8,128)S(1)}) fusion(f32[192,1536]{1,0:T(8,128)S(1)} %bitcast.98, bf16[192,1280]{1,0:T(8,128)(2,1)S(1)} %bitcast.87, bf16[1280,1536]{1,0:T(8,128)(2,1)} %all-gather.3.cloned.1.call-done), kind=kOutput, calls=%fused_computation.33 | convolution fusion | flops 756153984 | bytes 6784512 | tf_op jit(solution)/shard_map/dot_general | solution.py:73
  125.4 2.4 %fusion.26 = f32[192,1280]{1,0:T(8,128)} fusion(bf16[1280,1536]{1,0:T(8,128)(2,1)S(1)} %copy-done.2, f32[192,1536]{1,0:T(8,128)S(1)} %bitcast.99, f32[192,1536]{1,0:T(8,128)S(1)} %get-tuple-element.37, f32[192]{0:T(256)S(1)} %mul.105, f32[192]{0:T(256)S(1)} %get-tuple-element.14, f32[192]{0:T(256)S(1)} %get-tuple-element.27, f32[192]{0:T(256)S(1)} %get-tuple-element.13), kind=kOutput, calls=%fused_computation.26 | convolution fusion | flops 757235712 | bytes 7277568 | tf_op jit(solution)/shard_map/dot_general | solution.py:83
  127.8 5.7 %fusion.16 = bf16[192,1280]{1,0:T(8,128)(2,1)} fusion(f32[192,1280]{1,0:T(8,128)} %fusion.26, bf16[1280,1280]{1,0:T(8,128)(2,1)} %all-gather.5.cloned.1.call-done, f32[192,1280]{1,0:T(8,128)S(1)} %bitcast.100, bf16[192,1280]{1,0:T(8,128)(2,1)S(1)} %bitcast.88, f32[192]{0:T(256)S(1)} %mul.110), kind=kOutput, calls=%fused_computation.21 | convolution fusion | flops 1260257280 | bytes 6226688 | tf_op jit(solution)/shard_map/dot_general | solution.py:93
  (70 shorter events, 4.9 us)
Async XLA Ops:
  6.5 115.5 %copy-start = (bf16[12,2,8,1280]{3,2,1,0:T(8,128)(2,1)S(1)}, bf16[12,2,8,1280]{3,2,1,0:T(8,128)(2,1)}, u32[]{:S(2)}) copy-start(bf16[12,2,8,1280]{3,2,1,0:T(8,128)(2,1)} %param.12) | copy-start | bytes 1474564
  6.5 13.7 %copy-start.3 = (bf16[6,4,16,1280]{3,2,1,0:T(8,128)(2,1)S(1)}, bf16[6,4,16,1280]{3,2,1,0:T(8,128)(2,1)}, u32[]{:S(2)}) copy-start(bf16[6,4,16,1280]{3,2,1,0:T(8,128)(2,1)} %param.14) | copy-start | bytes 2949124
  6.5 115.5 %all-gather.3.cloned.1.call-start = ((), (), s32[]{:S(2)}) async-start(), calls=%async_computation.2 | async-start | bytes 4915200 | tf_op jit(solution)/shard_map/all_gather | solution.py:132
  13.6 13.0 %all-to-all-start = ((bf16[16,1,4,1536]{3,2,1,0:T(4,128)(2,1)}), bf16[16,1,4,1536]{3,2,1,0:T(4,128)(2,1)S(1)}, u32[]{:S(2)}, u32[]{:S(2)}) async-start(bf16[16,1,4,1536]{3,2,1,0:T(4,128)(2,1)} %bitcast.2), calls=%async_computation | async-start | bytes 393216 | tf_op jit(solution)/shard_map/all_to_all | solution.py:151
  26.7 6.1 %copy-start.7 = (s32[8]{0:T(128)S(1)}, s32[8]{0:T(128)}, u32[]{:S(2)}) copy-start(s32[8]{0:T(128)} %param.21) | copy-start | bytes 100
  26.7 6.2 %copy-start.6 = (f32[8,4]{0,1:T(4,128)S(1)}, f32[8,4]{0,1:T(4,128)}, u32[]{:S(2)}) copy-start(f32[8,4]{0,1:T(4,128)} %param.22) | copy-start | bytes 388
  26.7 62.2 %all-to-all-start.1 = ((bf16[16,4,16,1280]{3,2,1,0:T(8,128)(2,1)}), bf16[16,4,16,1280]{3,2,1,0:T(8,128)(2,1)S(1)}, u32[]{:S(2)}, u32[]{:S(2)}) async-start(bf16[16,4,16,1280]{3,2,1,0:T(8,128)(2,1)} %bitcast.43), calls=%async_computation.1 | async-start | bytes 5242880 | tf_op jit(solution)/shard_map/all_to_all | solution.py:166
  30.9 96.9 %all-gather.5.cloned.1.call-start = ((), (), s32[]{:S(2)}) async-start(), calls=%async_computation.3 | async-start | bytes 4096000 | tf_op jit(solution)/shard_map/all_gather | solution.py:133
  33.9 66.5 %collective-permute-start = (bf16[12,1,4,1536]{3,2,1,0:T(4,128)(2,1)}, bf16[12,1,4,1536]{3,2,1,0:T(4,128)(2,1)}, u32[]{:S(2)}, u32[]{:S(2)}) collective-permute-start(bf16[12,1,4,1536]{3,2,1,0:T(4,128)(2,1)} %bitcast.3), channel_id=1, source_target_pairs={{0,1},{1,2},{2,3},{4,5},{5,6},{6,7},{8,9},{9,10},{10,11},{12,13},{... | collective-permute-start | bytes 442376 | tf_op jit(solution)/shard_map/ppermute | solution.py:17
  38.7 61.8 %collective-permute-start.1 = (bf16[12,1,4,1536]{3,2,1,0:T(4,128)(2,1)}, bf16[12,1,4,1536]{3,2,1,0:T(4,128)(2,1)}, u32[]{:S(2)}, u32[]{:S(2)}) collective-permute-start(bf16[12,1,4,1536]{3,2,1,0:T(4,128)(2,1)} %bitcast.3), channel_id=1, source_target_pairs={{1,0},{2,1},{3,2},{5,4},{6,5},{7,6},{9,8},{10,9},{11,10},{13,12},{... | collective-permute-start | bytes 442376 | tf_op jit(solution)/shard_map/ppermute | solution.py:18
  91.8 8.7 %copy-start.5 = (f32[8,4]{0,1:T(4,128)S(1)}, f32[8,4]{0,1:T(4,128)}, u32[]{:S(2)}) copy-start(f32[8,4]{0,1:T(4,128)} %param.20) | copy-start | bytes 388
  91.8 10.7 %copy-start.4 = (f32[8,3]{0,1:T(4,128)S(1)}, f32[8,3]{0,1:T(4,128)}, u32[]{:S(2)}) copy-start(f32[8,3]{0,1:T(4,128)} %param.19) | copy-start | bytes 292
  92.9 16.9 %collective-permute-start.2 = (bf16[12,2,16,1280]{3,2,1,0:T(8,128)(2,1)}, bf16[12,2,16,1280]{3,2,1,0:T(8,128)(2,1)}, u32[]{:S(2)}, u32[]{:S(2)}) collective-permute-start(bf16[12,2,16,1280]{3,2,1,0:T(8,128)(2,1)} %get-tuple-element.17), channel_id=1, source_target_pairs={{0,1},{1,2},{2,3},{4,5},{5,6},{6,7},{8,9},{9,10},{10,11},{12,13},{... | collective-permute-start | bytes 2949128 | tf_op jit(solution)/shard_map/ppermute | solution.py:17
  98.5 15.5 %collective-permute-start.3 = (bf16[12,2,16,1280]{3,2,1,0:T(8,128)(2,1)S(1)}, bf16[12,2,16,1280]{3,2,1,0:T(8,128)(2,1)}, u32[]{:S(2)}, u32[]{:S(2)}) collective-permute-start(bf16[12,2,16,1280]{3,2,1,0:T(8,128)(2,1)S(1)} %get-tuple-element.18), channel_id=1, source_target_pairs={{1,0},{2,1},{3,2},{5,4},{6,5},{7,6},{9,8},{10,9},{11,10},{13,12},{... | collective-permute-start | bytes 2949128 | tf_op jit(solution)/shard_map/ppermute | solution.py:18
  102.5 11.5 %copy-start.8 = (f32[8,16]{1,0:T(8,128)S(1)}, f32[8,16]{1,0:T(8,128)}, u32[]{:S(2)}) copy-start(f32[8,16]{1,0:T(8,128)} %param.23) | copy-start | bytes 1540
  117.5 4.6 %copy-start.1 = (f32[12,2,8,1536]{3,2,1,0:T(8,128)S(1)}, f32[12,2,8,1536]{3,2,1,0:T(8,128)}, u32[]{:S(2)}) copy-start(f32[12,2,8,1536]{3,2,1,0:T(8,128)} %copy.86) | copy-start | bytes 3538948
  122.0 3.4 %copy-start.2 = (bf16[1280,1536]{1,0:T(8,128)(2,1)S(1)}, bf16[1280,1536]{1,0:T(8,128)(2,1)}, u32[]{:S(2)}) copy-start(bf16[1280,1536]{1,0:T(8,128)(2,1)} %all-gather.3.cloned.1.call-done) | copy-start | bytes 11796484
Sparse Core Ops, SparseCore 0:
  8.9 35.4 all-gather.2
  46.0 29.8 all-gather.4
where the time goes:
time: 141 us; the launch traced here: 140 us
  waiting for transfers between devices  57 us (40%)
  matrix products  29.7 us (21%)
  starting transfers between devices  24.8 us (18%)
  between operations  13.7 us (10%)
  local copies, waits for them, and re-layouts  11.9 us (8%)
  other arithmetic  3.19 us (2%)
    all_to_all x1, waiting for transfers between devices, sam_carry(): lax.all_to_all(values, 'img', split_axis=0, concat_axis=0, tiled=True)  48.2 us
    ppermute x2, starting transfers between devices, padded_2(): before = lax.ppermute(last, axis, up)  10.3 us
    dot_general x2, matrix products, resample_rows(): result = jnp.einsum('yk,bkxc->byxc', row_local, across, precision=HIGHEST)  10 us
    all_to_all x1, starting transfers between devices, dino_carry(): lax.all_to_all(values, 'img', split_axis=0, concat_axis=0, tiled=True)  6.35 us
    unnamed x25, local copies, waits for them, and re-layouts  5.77 us
    dot_general x1, matrix products, smooth_back(): lax.dot_general(delta, weight, (((1,), (1,)), ((), ())), preferred_elemen...  5.74 us
    dot_general x2, matrix products, resample_rows(): jnp.einsum('xj,bkjc->bkxc', col_weight, padded.astype(jnp.float32), preci...  5.49 us
    all_to_all x1, starting transfers between devices, sam_carry(): lax.all_to_all(values, 'img', split_axis=0, concat_axis=0, tiled=True)  4.27 us
  transfers between devices with their start and end apart: 8, of which 4 were waited for; matrix products, arithmetic and copies ran while one was open for 28% of the time, Pallas kernels for 0%

commit v1 on v0

v1 whole, which is shorter than its diff:
```python
import functools

import jax
import jax.numpy as jnp
from jax import lax
from jax.experimental import pallas as pl
from jax.experimental.pallas import tpu as pltpu
from jax.sharding import PartitionSpec as P

EPSILON = 1e-06
BF16 = jnp.bfloat16
F32 = jnp.float32
SMEM = pl.BlockSpec(memory_space=pltpu.SMEM)
VMEM = pl.BlockSpec(memory_space=pltpu.VMEM)
ANY = pl.BlockSpec(memory_space=pl.ANY)
VMEM_BYTES = 48 * 1024 * 1024


def params():
    return pltpu.CompilerParams(vmem_limit_bytes=VMEM_BYTES)


def split_dot(matrix, values):
    rows = matrix.shape[0]
    high = matrix.astype(BF16)
    low = (matrix - high.astype(F32)).astype(BF16)
    both = jnp.concatenate([high, low], axis=0)
    product = jnp.dot(both, values, preferred_element_type=F32)
    return product[:rows] + product[rows:]


def own_rows(list_ref, first, per_device, image_dev, capacity):
    owners = [lax.div(list_ref[first + i], image_dev) for i in range(per_device)]
    rows = []
    for i in range(per_device):
        position = jnp.int32(0)
        for j in range(i):
            position = position + jnp.where(owners[j] == owners[i], 1, 0)
        rows.append(owners[i] * capacity + position)
    return rows


def arrived_rows(list_ref, rank, slots, per_device, image_dev, capacity, row_of):
    for k in range(image_dev):
        row_of[k] = -1

    def source(peer, _):
        def slot(i, seen):
            image = list_ref[peer * per_device + i]
            mine = lax.div(image, image_dev) == rank

            @pl.when(mine)
            def _():
                row_of[image - rank * image_dev] = peer * capacity + seen

            return seen + jnp.where(mine, 1, 0)

        lax.fori_loop(0, per_device, slot, jnp.int32(0), unroll=True)
        return 0

    lax.fori_loop(0, slots // per_device, source, 0)


def pre_kernel(
    dims,
    dino_list,
    sam_list,
    start,
    row_weight,
    col_weight,
    dino_feats,
    sam_feats,
    dino_pack,
    own,
    core_part,
    edge_part,
):
    per_device, image_dev, capacity, grid_rows = dims
    rank = lax.axis_index("img")
    sp = lax.axis_index("sp")
    dino_pack[...] = jnp.zeros_like(dino_pack)
    for i, row in enumerate(own_rows(dino_list, rank * per_device, per_device, image_dev, capacity)):
        dino_pack[row] = dino_feats[i]

    even = lax.rem(sp, 2) == 0
    up, down = 2 * sp - 1, 2 * sp + 2
    targets = [2 * sp, 2 * sp + 1, jnp.where(even, down, up), jnp.where(even, up, down)]
    col_count = col_weight.shape[1]
    across = jnp.concatenate([col_weight[...]] * 4, axis=1)
    column_row = lax.broadcasted_iota(jnp.int32, across.shape, 1) // col_count
    blocks = []
    for y in targets:
        inside = jnp.logical_and(y >= 0, y < grid_rows)
        line = jnp.clip(y, 0, grid_rows - 1)
        first = start[line] - 4 * sp
        taps = jnp.zeros(across.shape, F32)
        for tap in range(row_weight.shape[1]):
            weight = jnp.where(inside, row_weight[line, tap], 0.0)
            taps = taps + jnp.where(column_row == first + tap, weight, 0.0)
        blocks.append(across * taps)
    matrix = jnp.concatenate(blocks, axis=0)
    wide = own.shape[1]
    half = wide // 2
    for i in range(per_device):
        result = split_dot(matrix, sam_feats[i])
        own[i] = result[:wide]
        core_part[i] = result[wide : wide + half].astype(BF16)
        edge_part[i] = result[wide + half :].astype(BF16)


def pack_kernel(dims, sam_list, own, core_part, edge_part, packed):
    per_device, image_dev, capacity = dims
    rank = lax.axis_index("img")
    even = lax.rem(lax.axis_index("sp"), 2) == 0
    half = core_part.shape[1]
    rows = own_rows(sam_list, rank * per_device, per_device, image_dev, capacity)
    for i, row in enumerate(rows):
        core = core_part[i].astype(F32)
        edge = edge_part[i].astype(F32)
        top = own[i, :half] + jnp.where(even, edge, core)
        bottom = own[i, half:] + jnp.where(even, core, edge)
        packed[row] = jnp.concatenate([top, bottom], axis=0).astype(BF16)


def target_kernel(
    dims, dino_list, row_weight, col_weight, here, core_side, edge_side, target, stacked, row_of
):
    slots, per_device, image_dev, capacity = dims
    rank = lax.axis_index("img")
    sp = lax.axis_index("sp")
    even = lax.rem(sp, 2) == 0
    arrived_rows(dino_list, rank, slots, per_device, image_dev, capacity, row_of)
    buffer_rows, cols = here.shape[0], here.shape[1]
    for b in range(buffer_rows):
        core = core_side[b].astype(F32)
        edge = edge_side[b].astype(F32)
        above = jnp.where(even, edge, core)
        below = jnp.where(even, core, edge)
        for k, values in enumerate((above, here[b].astype(F32), below)):
            at = (k * buffer_rows + b) * cols
            stacked[at : at + cols, :] = values
    values = stacked[...].astype(BF16)
    patch_cols = col_weight.shape[0]
    shape = (patch_cols, 3 * buffer_rows * cols)
    column = lax.broadcasted_iota(jnp.int32, shape, 1)
    tap_of = column // (buffer_rows * cols)
    row_at = (column // cols) % buffer_rows
    j_of = column % cols
    across = jnp.zeros(shape, F32)
    for j in range(cols):
        across = across + jnp.where(j_of == j, col_weight[:, j : j + 1], 0.0)
    lines = []
    for y in range(2):
        taps = jnp.zeros(shape, F32)
        for k in range(3):
            taps = taps + jnp.where(tap_of == k, row_weight[2 * sp + y, k], 0.0)
        lines.append(across * taps)
    base = jnp.concatenate(lines, axis=0)
    row_at = jnp.concatenate([row_at] * 2, axis=0)
    matrix = jnp.concatenate(
        [jnp.where(row_at == row_of[k], base, 0.0) for k in range(image_dev)], axis=0
    )
    target[...] = split_dot(matrix, values).astype(BF16)


def load_pieces(pieces, offsets, whole, sems):
    copies = []
    for n, (piece, offset) in enumerate(zip(pieces, offsets)):
        rows = piece.shape[0]
        place = pl.ds(pl.multiple_of(offset, 16), rows)
        copies.append(pltpu.make_async_copy(piece, whole.at[place, :], sems.at[n]))
    for copy in copies:
        copy.start()
    for copy in copies:
        copy.wait()


def piece_offsets(count, rows):
    if count == 1:
        return [0]
    sp = lax.axis_index("sp")
    half = jnp.where(sp >= 2, 2, 0)
    core = lax.rem(sp, 2)
    order = (half + core, half + 1 - core, 2 - half + core, 2 - half + 1 - core)
    return [o * rows for o in order]


def row_sum(values):
    return jnp.sum(values, axis=-1, keepdims=True)


def dino_kernel(count, student, target, *rest):
    pieces, (grad, whole, predicted, delta, sems) = rest[:count], rest[count:]
    load_pieces(pieces, piece_offsets(count, pieces[0].shape[0]), whole, sems)
    predicted[...] = jnp.dot(student[...], whole[...], preferred_element_type=F32)
    p = predicted[...]
    t = target[...].astype(F32)
    pred_inv = 1.0 / jnp.sqrt(row_sum(p * p) + EPSILON)
    goal_inv = 1.0 / jnp.sqrt(row_sum(t * t) + EPSILON)
    cosine = row_sum(p * t) * pred_inv * goal_inv
    features = p.shape[-1]
    delta[...] = (
        (features * pred_inv) * ((cosine * pred_inv) * p - goal_inv * t)
    ).astype(BF16)
    grad[...] = lax.dot_general(
        delta[...], whole[...], (((1,), (1,)), ((), ())), preferred_element_type=F32
    ).astype(BF16)


def sam_kernel(count, dims, sam_list, student, arrived, dino_grad, *rest):
    slots, per_device, image_dev, capacity = dims
    pieces, (out, whole, delta, row_of, sems) = rest[:count], rest[count:]
    rank = lax.axis_index("img")
    arrived_rows(sam_list, rank, slots, per_device, image_dev, capacity, row_of)
    load_pieces(pieces, piece_offsets(count, pieces[0].shape[0]), whole, sems)
    predicted = jnp.dot(student[...], whole[...], preferred_element_type=F32)
    patch = arrived.shape[1]
    for k in range(image_dev):
        row = row_of[k]
        target = arrived[jnp.maximum(row, 0)].astype(F32)
        error = jnp.clip(predicted[k * patch : (k + 1) * patch] - target, -1.0, 1.0)
        delta[k * patch : (k + 1) * patch, :] = jnp.where(row >= 0, error, 0.0).astype(BF16)
    back = lax.dot_general(
        delta[...], whole[...], (((1,), (1,)), ((), ())), preferred_element_type=F32
    )
    total = back.astype(BF16).astype(F32) + dino_grad[...].astype(F32)
    out[...] = total.astype(BF16)


def pair_perms(count):
    core = [(i, i ^ 1) for i in range(count)]
    edge = []
    for i in range(1, count - 1, 2):
        edge += [(i, i + 1), (i + 1, i)]
    return core, edge


def shards(
    student,
    dino_feats,
    sam_feats,
    dino_proj,
    sam_proj,
    dino_list,
    sam_list,
    dino_row_weight,
    dino_col_weight,
    sam_start,
    sam_row_weight,
    sam_col_weight,
):
    peers = lax.axis_size("img")
    sp_count = lax.axis_size("sp")
    images, rows_dev, patch_cols, width = student.shape
    slots = dino_list.shape[0]
    per_device = slots // peers
    capacity = (2 * per_device + peers - 1) // peers
    buffer_rows = peers * capacity
    patch = rows_dev * patch_cols
    grid_rows = dino_row_weight.shape[0]
    dino_cols, dino_width = dino_feats.shape[2:]
    sam_rows, sam_cols, sam_width = sam_feats.shape[1:]
    core_perm, edge_perm = pair_perms(sp_count)

    def core_swap(values):
        return lax.ppermute(values, "sp", core_perm)

    def edge_swap(values):
        return lax.ppermute(values, "sp", edge_perm)

    half_shape = jax.ShapeDtypeStruct((per_device, patch_cols, sam_width), BF16)
    dino_pack, own, core_part, edge_part = pl.pallas_call(
        functools.partial(pre_kernel, (per_device, images, capacity, grid_rows)),
        out_shape=(
            jax.ShapeDtypeStruct((buffer_rows, dino_cols, dino_width), BF16),
            jax.ShapeDtypeStruct((per_device, patch, sam_width), F32),
            half_shape,
            half_shape,
        ),
        in_specs=[SMEM] * 4 + [VMEM] * 3,
        out_specs=(VMEM,) * 4,
        compiler_params=params(),
        name="pre",
    )(
        dino_list,
        sam_list,
        sam_start,
        sam_row_weight,
        sam_col_weight,
        dino_feats.reshape(per_device, dino_cols, dino_width),
        sam_feats.reshape(per_device, sam_rows * sam_cols, sam_width),
    )

    edge_got = edge_swap(edge_part)
    core_got = core_swap(core_part)
    dino_got = lax.all_to_all(dino_pack, "img", split_axis=0, concat_axis=0, tiled=True)

    sam_pack = pl.pallas_call(
        functools.partial(pack_kernel, (per_device, images, capacity)),
        out_shape=jax.ShapeDtypeStruct((buffer_rows, patch, sam_width), BF16),
        in_specs=[SMEM] + [VMEM] * 3,
        out_specs=VMEM,
        compiler_params=params(),
        name="pack",
    )(sam_list, own, core_got, edge_got)
    sam_got = lax.all_to_all(sam_pack, "img", split_axis=0, concat_axis=0, tiled=True)

    dino_core, dino_edge = core_swap(dino_got), edge_swap(dino_got)
    if sp_count == 4:
        chip_perm = [(i, i ^ 2) for i in range(4)]

        def gather(shard):
            across = lax.ppermute(shard, "sp", chip_perm)
            return [shard, core_swap(shard), across, core_swap(across)]

        dino_pieces, sam_pieces = gather(dino_proj), gather(sam_proj)
    else:
        dino_pieces = [lax.all_gather(dino_proj, "sp", axis=0, tiled=True)]
        sam_pieces = [lax.all_gather(sam_proj, "sp", axis=0, tiled=True)]

    target = pl.pallas_call(
        functools.partial(target_kernel, (slots, per_device, images, capacity)),
        out_shape=jax.ShapeDtypeStruct((images * patch, dino_width), BF16),
        in_specs=[SMEM, SMEM] + [VMEM] * 4,
        out_specs=VMEM,
        scratch_shapes=[
            pltpu.VMEM((3 * buffer_rows * dino_cols, dino_width), F32),
            pltpu.SMEM((images,), jnp.int32),
        ],
        compiler_params=params(),
        name="target",
    )(dino_list, dino_row_weight, dino_col_weight, dino_got, dino_core, dino_edge)

    rows = student.reshape(images * patch, width)
    count = len(dino_pieces)
    dino_grad = pl.pallas_call(
        functools.partial(dino_kernel, count),
        out_shape=jax.ShapeDtypeStruct(rows.shape, BF16),
        in_specs=[VMEM, VMEM] + [ANY] * count,
        out_specs=VMEM,
        scratch_shapes=[
            pltpu.VMEM((width, dino_width), BF16),
            pltpu.VMEM((rows.shape[0], dino_width), F32),
            pltpu.VMEM((rows.shape[0], dino_width), BF16),
            pltpu.SemaphoreType.DMA((count,)),
        ],
        compiler_params=params(),
        name="dino",
    )(rows, target, *dino_pieces)

    out = pl.pallas_call(
        functools.partial(sam_kernel, count, (slots, per_device, images, capacity)),
        out_shape=jax.ShapeDtypeStruct(rows.shape, BF16),
        in_specs=[SMEM] + [VMEM] * 3 + [ANY] * count,
        out_specs=VMEM,
        scratch_shapes=[
            pltpu.VMEM((width, sam_width), BF16),
            pltpu.VMEM((rows.shape[0], sam_width), BF16),
            pltpu.SMEM((images,), jnp.int32),
            pltpu.SemaphoreType.DMA((count,)),
        ],
        compiler_params=params(),
        name="sam",
    )(sam_list, rows, sam_got, dino_grad, *sam_pieces)
    return out.reshape(student.shape)


def solution(mesh):
    placed = (
        P("img", "sp", None, None),
        P("img", "sp", None, None),
        P("img", "sp", None, None),
        P("sp", None),
        P("sp", None),
        P(),
        P(),
        P(),
        P(),
        P(),
        P(),
        P(),
    )
    return jax.shard_map(
        shards, mesh=mesh, in_specs=placed, out_specs=P("img", "sp", None, None), check_vma=False
    )
```

time: 141 us -> 74.1 us (0.53)
  matrix products: 29.7 us -> 0 us
  waiting for transfers between devices: 57 us -> 31.9 us
  Pallas kernels: 0 us -> 14.4 us
  between operations: 13.7 us -> 0.14 us
  local copies, waits for them, and re-layouts: 11.9 us -> 3.71 us
  other arithmetic: 3.19 us -> 0 us
    all_to_all x2, waiting for transfers between devices: 51.2 us -> 0.01 us  [the longest x1 0.01 us: shards(): lax.all_to_all(dino_pack, 'img', split_axis=0, concat_axis=0, tiled=True)]
    dot_general x13 -> x0, matrix products: 29.7 us -> none  [the longest x2 10 us: resample_rows(): result = jnp.einsum('yk,bkxc->byxc', row_local, across, precision=HIGHEST)]
    ppermute x4 -> x10, waiting for transfers between devices: 4.4 us -> 31.9 us  [the longest x2 29.1 us: edge_swap(): return lax.ppermute(values, 'sp', edge_perm)]
    pallas_call x0 -> x5, Pallas kernels: none -> 14.4 us  [the longest x1 5.19 us: shards(): pl.pallas_call(functools.partial(sam_kernel, count, (slots, per_device, i...]
    ppermute x4 -> x10, starting transfers between devices: 14.2 us -> 11.8 us  [the longest x2 7.03 us: edge_swap(): return lax.ppermute(values, 'sp', edge_perm)]
    unnamed x25, local copies, waits for them, and re-layouts: 5.77 us -> 3.71 us
    reshape x2 -> x0, local copies, waits for them, and re-layouts: 1.56 us -> none  [apply_rows(): return product.reshape((matrix.shape[0],) + values.shape[1:])]
  transfers between devices with their start and end apart: 8 -> 12, of which waited for: 4 -> 3; matrix products, arithmetic and copies ran while one was open for 28% -> 1% of each run, Pallas kernels for 0% -> 13%
where the time goes in v1:
time: 74.1 us; the launch traced here: 73.6 us
  waiting for transfers between devices  31.9 us (43%)
  starting transfers between devices  23.4 us (32%)
  Pallas kernels  14.4 us (19%)
  local copies, waits for them, and re-layouts  3.71 us (5%)
    ppermute x2, waiting for transfers between devices, edge_swap(): return lax.ppermute(values, 'sp', edge_perm)  29.1 us
    ppermute x2, starting transfers between devices, edge_swap(): return lax.ppermute(values, 'sp', edge_perm)  7.03 us
    all_to_all x1, starting transfers between devices, shards(): lax.all_to_all(sam_pack, 'img', split_axis=0, concat_axis=0, tiled=True)  5.89 us
    all_to_all x1, starting transfers between devices, shards(): lax.all_to_all(dino_pack, 'img', split_axis=0, concat_axis=0, tiled=True)  5.69 us
    pallas_call x1, Pallas kernels, shards(): pl.pallas_call(functools.partial(sam_kernel, count, (slots, per_device, i...  5.19 us
    pallas_call x1, Pallas kernels, shards(): pl.pallas_call(functools.partial(dino_kernel, count), out_shape=jax.Shape...  4.58 us
    unnamed x25, local copies, waits for them, and re-layouts  3.71 us
    ppermute x6, waiting for transfers between devices, core_swap(): return lax.ppermute(values, 'sp', core_perm)  2.8 us
  transfers between devices with their start and end apart: 12, of which 3 were waited for; matrix products, arithmetic and copies ran while one was open for 1% of the time, Pallas kernels for 13%

profile of v1, /device:TPU:1, one launch (start us, length us, event | category | flops | bytes accessed | tf_op | source)
XLA Modules:
  0.0 73.6 jit_solution(5902263095412220150)
XLA Ops:
  0.0 2.1 %collective-permute-start.5 = (bf16[320,1536]{1,0:T(8,128)(2,1)}, bf16[320,1536]{1,0:T(8,128)(2,1)}, u32[]{:S(2)}, u32[]{:S(2)}) collective-permute-start(bf16[320,1536]{1,0:T(8,128)(2,1)} %rest_0_.2), channel_id=1, source_target_pairs={{0,2},{1,3},{2,0},{3,1},{4,6},{5,7},{6,4},{7,5},{8,10},{9,11},{10,... | collective-permute-start | bytes 2949128 | tf_op jit(solution)/shard_map/ppermute | solution.py:313
  2.1 0.1 collective-permute-start.8
  2.1 0.8 %copy.13.row_weight = f32[8,4]{1,0:T(8,128)S(1)} copy(f32[8,4]{0,1:T(4,128)} %param.22) | data formatting | bytes 256 | tf_op args[10]
  2.9 0.6 copy-done.5
  3.5 0.0 copy-done.7
  3.6 0.0 copy-done.8
  3.6 1.2 %copy-done.1 = bf16[6,4,16,1280]{3,2,1,0:T(8,128)(2,1)S(1)} copy-done((bf16[6,4,16,1280]{3,2,1,0:T(8,128)(2,1)S(1)}, bf16[6,4,16,1280]{3,2,1,0:T(8,128)(2,1)}, u32[]{:S(2)}) %copy-start.1) | copy-done | bytes 983064
  4.8 0.9 %copy-done.4 = bf16[6,1,4,1536]{3,2,1,0:T(4,128)(2,1)S(1)} copy-done((bf16[6,1,4,1536]{3,2,1,0:T(4,128)(2,1)S(1)}, bf16[6,1,4,1536]{3,2,1,0:T(4,128)(2,1)}, u32[]{:S(2)}) %copy-start.4) | copy-done | bytes 73752
  5.7 1.4 %pre.1 = (bf16[16,4,1536]{2,1,0:T(4,128)(2,1)}, f32[6,16,1280]{2,1,0:T(8,128)S(1)}, bf16[6,8,1280]{2,1,0:T(8,128)(2,1)S(1)}, bf16[6,8,1280]{2,1,0:T(8,128)(2,1)S(1)}) custom-call(s32[48]{0:T(128)S(1)} %copy-done.7, s32[48]{0:T(128)S(1)} %copy-done.5, s32[8]{0:T(128)S(1)} %copy-done.8, f32[8,4]{1,0:T(8,128)S(1)} %copy.13.row_weight, f32[8,16]{1,0:T(8,128)S(1)} %copy-done.6, ...), custom_call_target="tpu_custom_call" | custom-call | tf_op jit(solution)/shard_map/pre/pallas_call | solution.py:272
  7.0 5.7 %all-to-all-start.1 = ((bf16[16,4,1536]{2,1,0:T(4,128)(2,1)}), bf16[16,4,1536]{2,1,0:T(4,128)(2,1)S(1)}, u32[]{:S(2)}, u32[]{:S(2)}) async-start(bf16[16,4,1536]{2,1,0:T(4,128)(2,1)} %get-tuple-element.12), calls=%async_computation.1 | async-start | bytes 393216 | tf_op jit(solution)/shard_map/all_to_all | solution.py:296
  12.7 1.5 %collective-permute-start = (bf16[6,8,1280]{2,1,0:T(8,128)(2,1)S(1)}, bf16[6,8,1280]{2,1,0:T(8,128)(2,1)S(1)}, u32[]{:S(2)}, u32[]{:S(2)}) collective-permute-start(bf16[6,8,1280]{2,1,0:T(8,128)(2,1)S(1)} %get-tuple-element.10), channel_id=1, source_target_pairs={{0,1},{1,0},{2,3},{3,2},{4,5},{5,4},{6,7},{7,6},{8,9},{9,8},{10,11... | collective-permute-start | bytes 368648 | tf_op jit(solution)/shard_map/ppermute | solution.py:266
  14.2 3.0 %collective-permute-start.1 = (bf16[6,8,1280]{2,1,0:T(8,128)(2,1)S(1)}, bf16[6,8,1280]{2,1,0:T(8,128)(2,1)S(1)}, u32[]{:S(2)}, u32[]{:S(2)}) collective-permute-start(bf16[6,8,1280]{2,1,0:T(8,128)(2,1)S(1)} %get-tuple-element.11), channel_id=1, source_target_pairs={{1,2},{2,1},{5,6},{6,5},{9,10},{10,9},{13,14},{14,13},{17,18},{18,... | collective-permute-start | bytes 368648 | tf_op jit(solution)/shard_map/ppermute | solution.py:269
  17.3 0.0 collective-permute-done.core_part
  17.3 25.9 %collective-permute-done.1.edge_part = bf16[6,8,1280]{2,1,0:T(8,128)(2,1)S(1)} collective-permute-done((bf16[6,8,1280]{2,1,0:T(8,128)(2,1)S(1)}, bf16[6,8,1280]{2,1,0:T(8,128)(2,1)S(1)}, u32[]{:S(2)}, u32[]{:S(2)}) %collective-permute-start.1) | collective-permute-done | bytes 122912 | tf_op jit(solution)/shard_map/ppermute | solution.py:269
  43.2 1.5 %pack.1 = bf16[16,16,1280]{2,1,0:T(8,128)(2,1)} custom-call(s32[48]{0:T(128)S(1)} %copy-done.5, f32[6,16,1280]{2,1,0:T(8,128)S(1)} %get-tuple-element.9.own, bf16[6,8,1280]{2,1,0:T(8,128)(2,1)S(1)} %collective-permute-done.core_part, bf16[6,8,1280]{2,1,0:T(8,128)(2,1)S(1)} %collective-permute-done.1.edge_part), custom_call_target="tpu_custom_call" | custom-call | tf_op jit(solution)/shard_map/pack/pallas_call | solution.py:298
  44.7 0.0 all-to-all-done.1.here
  44.7 5.9 %all-to-all-start = ((bf16[16,16,1280]{2,1,0:T(8,128)(2,1)}), bf16[16,16,1280]{2,1,0:T(8,128)(2,1)S(1)}, u32[]{:S(2)}, u32[]{:S(2)}) async-start(bf16[16,16,1280]{2,1,0:T(8,128)(2,1)} %pack.1), calls=%async_computation | async-start | bytes 1310720 | tf_op jit(solution)/shard_map/all_to_all | solution.py:306
  50.5 0.0 copy-start.10
  50.6 0.1 collective-permute-start.4
  50.7 0.5 collective-permute-start.6
  51.1 0.1 collective-permute-start.7
  51.2 0.0 collective-permute-done.8.rest_2_
  51.2 0.4 collective-permute-start.9
  51.7 0.1 collective-permute-start.2
  51.7 2.8 %collective-permute-done.2.core_side = bf16[16,4,1536]{2,1,0:T(4,128)(2,1)S(1)} collective-permute-done((bf16[16,4,1536]{2,1,0:T(4,128)(2,1)S(1)}, bf16[16,4,1536]{2,1,0:T(4,128)(2,1)S(1)}, u32[]{:S(2)}, u32[]{:S(2)}) %collective-permute-start.2) | collective-permute-done | bytes 196640 | tf_op jit(solution)/shard_map/ppermute | solution.py:266
  54.5 4.0 %collective-permute-start.3 = (bf16[16,4,1536]{2,1,0:T(4,128)(2,1)S(1)}, bf16[16,4,1536]{2,1,0:T(4,128)(2,1)}, u32[]{:S(2)}, u32[]{:S(2)}) collective-permute-start(bf16[16,4,1536]{2,1,0:T(4,128)(2,1)S(1)} %all-to-all-done.1.here), channel_id=1, source_target_pairs={{1,2},{2,1},{5,6},{6,5},{9,10},{10,9},{13,14},{14,13},{17,18},{18,... | collective-permute-start | bytes 589832 | tf_op jit(solution)/shard_map/ppermute | solution.py:269
  58.5 0.1 copy.14.row_weight
  58.6 0.1 copy.15.col_weight
  58.7 3.3 %collective-permute-done.3.edge_side = bf16[16,4,1536]{2,1,0:T(4,128)(2,1)} collective-permute-done((bf16[16,4,1536]{2,1,0:T(4,128)(2,1)S(1)}, bf16[16,4,1536]{2,1,0:T(4,128)(2,1)}, u32[]{:S(2)}, u32[]{:S(2)}) %collective-permute-start.3) | collective-permute-done | bytes 196640 | tf_op jit(solution)/shard_map/ppermute | solution.py:269
  62.0 1.8 %target.1 = bf16[192,1536]{1,0:T(8,128)(2,1)S(1)} custom-call(s32[48]{0:T(128)S(1)} %copy-done.7, f32[8,3]{1,0:T(8,128)S(1)} %copy.14.row_weight, f32[8,4]{1,0:T(8,128)S(1)} %copy.15.col_weight, bf16[16,4,1536]{2,1,0:T(4,128)(2,1)S(1)} %all-to-all-done.1.here, bf16[16,4,1536]{2,1,0:T(4,128)(2,1)S(1)} %collective-permute-done.2.core_side, ...), custom_call_target="tpu_custom_call" | custom-call | tf_op jit(solution)/shard_map/target/pallas_call | solution.py:321
  63.8 4.6 %dino.1.dino_grad = bf16[192,1280]{1,0:T(8,128)(2,1)S(1)} custom-call(bf16[192,1280]{1,0:T(8,128)(2,1)S(1)} %bitcast.4, bf16[192,1536]{1,0:T(8,128)(2,1)S(1)} %target.1, bf16[320,1536]{1,0:T(8,128)(2,1)S(1)} %copy-done.2, bf16[320,1536]{1,0:T(8,128)(2,1)} %collective-permute-done.4.rest_1_, bf16[320,1536]{1,0:T(8,128)(2,1)} %collective-permute-done.5.rest_2_, ...), custom_call_target="tpu_custom_call" | custom-call | tf_op jit(solution)/shard_map/dino/pallas_call | solution.py:336
  68.4 5.2 %sam.1 = bf16[192,1280]{1,0:T(8,128)(2,1)} custom-call(s32[48]{0:T(128)S(1)} %copy-done.5, bf16[192,1280]{1,0:T(8,128)(2,1)S(1)} %bitcast.5, bf16[16,16,1280]{2,1,0:T(8,128)(2,1)S(1)} %all-to-all-done.arrived, bf16[192,1280]{1,0:T(8,128)(2,1)S(1)} %dino.1.dino_grad, bf16[320,1280]{1,0:T(8,128)(2,1)S(1)} %copy-done.3, ...), custom_call_target="tpu_custom_call" | custom-call | tf_op jit(solution)/shard_map/sam/pallas_call | solution.py:351
  (22 shorter events, 0.0 us)
Async XLA Ops:
  0.0 2.9 %copy-start.6 = (f32[8,16]{1,0:T(8,128)S(1)}, f32[8,16]{1,0:T(8,128)}, u32[]{:S(2)}) copy-start(f32[8,16]{1,0:T(8,128)} %col_weight.2) | copy-start | bytes 1540
  0.0 50.6 %collective-permute-start.5 = (bf16[320,1536]{1,0:T(8,128)(2,1)}, bf16[320,1536]{1,0:T(8,128)(2,1)}, u32[]{:S(2)}, u32[]{:S(2)}) collective-permute-start(bf16[320,1536]{1,0:T(8,128)(2,1)} %rest_0_.2), channel_id=1, source_target_pairs={{0,2},{1,3},{2,0},{3,1},{4,6},{5,7},{6,4},{7,5},{8,10},{9,11},{10,... | collective-permute-start | bytes 2949128 | tf_op jit(solution)/shard_map/ppermute | solution.py:313
  2.1 49.2 %collective-permute-start.8 = (bf16[320,1280]{1,0:T(8,128)(2,1)}, bf16[320,1280]{1,0:T(8,128)(2,1)}, u32[]{:S(2)}, u32[]{:S(2)}) collective-permute-start(bf16[320,1280]{1,0:T(8,128)(2,1)} %rest_0_.3), channel_id=1, source_target_pairs={{0,2},{1,3},{2,0},{3,1},{4,6},{5,7},{6,4},{7,5},{8,10},{9,11},{10,... | collective-permute-start | bytes 2457608 | tf_op jit(solution)/shard_map/ppermute | solution.py:313
  2.9 0.7 copy-start.5
  2.9 0.7 copy-start.7
  2.9 0.7 copy-start.8
  3.6 1.2 %copy-start.1 = (bf16[6,4,16,1280]{3,2,1,0:T(8,128)(2,1)S(1)}, bf16[6,4,16,1280]{3,2,1,0:T(8,128)(2,1)}, u32[]{:S(2)}) copy-start(bf16[6,4,16,1280]{3,2,1,0:T(8,128)(2,1)} %param.14) | copy-start | bytes 2949124
  4.8 0.9 %copy-start.4 = (bf16[6,1,4,1536]{3,2,1,0:T(4,128)(2,1)S(1)}, bf16[6,1,4,1536]{3,2,1,0:T(4,128)(2,1)}, u32[]{:S(2)}) copy-start(bf16[6,1,4,1536]{3,2,1,0:T(4,128)(2,1)} %param.13) | copy-start | bytes 221188
  7.0 37.6 %all-to-all-start.1 = ((bf16[16,4,1536]{2,1,0:T(4,128)(2,1)}), bf16[16,4,1536]{2,1,0:T(4,128)(2,1)S(1)}, u32[]{:S(2)}, u32[]{:S(2)}) async-start(bf16[16,4,1536]{2,1,0:T(4,128)(2,1)} %get-tuple-element.12), calls=%async_computation.1 | async-start | bytes 393216 | tf_op jit(solution)/shard_map/all_to_all | solution.py:296
  12.7 4.6 %collective-permute-start = (bf16[6,8,1280]{2,1,0:T(8,128)(2,1)S(1)}, bf16[6,8,1280]{2,1,0:T(8,128)(2,1)S(1)}, u32[]{:S(2)}, u32[]{:S(2)}) collective-permute-start(bf16[6,8,1280]{2,1,0:T(8,128)(2,1)S(1)} %get-tuple-element.10), channel_id=1, source_target_pairs={{0,1},{1,0},{2,3},{3,2},{4,5},{5,4},{6,7},{7,6},{8,9},{9,8},{10,11... | collective-permute-start | bytes 368648 | tf_op jit(solution)/shard_map/ppermute | solution.py:266
  14.2 28.9 %collective-permute-start.1 = (bf16[6,8,1280]{2,1,0:T(8,128)(2,1)S(1)}, bf16[6,8,1280]{2,1,0:T(8,128)(2,1)S(1)}, u32[]{:S(2)}, u32[]{:S(2)}) collective-permute-start(bf16[6,8,1280]{2,1,0:T(8,128)(2,1)S(1)} %get-tuple-element.11), channel_id=1, source_target_pairs={{1,2},{2,1},{5,6},{6,5},{9,10},{10,9},{13,14},{14,13},{17,18},{18,... | collective-permute-start | bytes 368648 | tf_op jit(solution)/shard_map/ppermute | solution.py:269
  43.2 8.0 %copy-start.3 = (bf16[320,1280]{1,0:T(8,128)(2,1)S(1)}, bf16[320,1280]{1,0:T(8,128)(2,1)}, u32[]{:S(2)}) copy-start(bf16[320,1280]{1,0:T(8,128)(2,1)} %rest_0_.3) | copy-start | bytes 2457604
  44.6 5.9 %copy-start.2 = (bf16[320,1536]{1,0:T(8,128)(2,1)S(1)}, bf16[320,1536]{1,0:T(8,128)(2,1)}, u32[]{:S(2)}) copy-start(bf16[320,1536]{1,0:T(8,128)(2,1)} %rest_0_.2) | copy-start | bytes 2949124
  44.7 13.9 %copy-start.9 = (f32[8,3]{0,1:T(4,128)S(1)}, f32[8,3]{0,1:T(4,128)}, u32[]{:S(2)}) copy-start(f32[8,3]{0,1:T(4,128)} %param.19) | copy-start | bytes 292
  44.7 23.8 %all-to-all-start = ((bf16[16,16,1280]{2,1,0:T(8,128)(2,1)}), bf16[16,16,1280]{2,1,0:T(8,128)(2,1)S(1)}, u32[]{:S(2)}, u32[]{:S(2)}) async-start(bf16[16,16,1280]{2,1,0:T(8,128)(2,1)} %pack.1), calls=%async_computation | async-start | bytes 1310720 | tf_op jit(solution)/shard_map/all_to_all | solution.py:306
  50.5 8.1 %copy-start.10 = (f32[8,4]{0,1:T(4,128)S(1)}, f32[8,4]{0,1:T(4,128)}, u32[]{:S(2)}) copy-start(f32[8,4]{0,1:T(4,128)} %param.20) | copy-start | bytes 388
  50.6 13.2 %collective-permute-start.4 = (bf16[320,1536]{1,0:T(8,128)(2,1)S(1)}, bf16[320,1536]{1,0:T(8,128)(2,1)}, u32[]{:S(2)}, u32[]{:S(2)}) collective-permute-start(bf16[320,1536]{1,0:T(8,128)(2,1)S(1)} %copy-done.2), channel_id=1, source_target_pairs={{0,1},{1,0},{2,3},{3,2},{4,5},{5,4},{6,7},{7,6},{8,9},{9,8},{10,11... | collective-permute-start | bytes 2949128 | tf_op jit(solution)/shard_map/ppermute | solution.py:266
  50.7 13.1 %collective-permute-start.6 = (bf16[320,1536]{1,0:T(8,128)(2,1)}, bf16[320,1536]{1,0:T(8,128)(2,1)}, u32[]{:S(2)}, u32[]{:S(2)}) collective-permute-start(bf16[320,1536]{1,0:T(8,128)(2,1)} %collective-permute-done.5.rest_2_), channel_id=1, source_target_pairs={{0,1},{1,0},{2,3},{3,2},{4,5},{5,4},{6,7},{7,6},{8,9},{9,8},{10,11... | collective-permute-start | bytes 2949128 | tf_op jit(solution)/shard_map/ppermute | solution.py:266
  51.1 17.3 %collective-permute-start.7 = (bf16[320,1280]{1,0:T(8,128)(2,1)S(1)}, bf16[320,1280]{1,0:T(8,128)(2,1)}, u32[]{:S(2)}, u32[]{:S(2)}) collective-permute-start(bf16[320,1280]{1,0:T(8,128)(2,1)S(1)} %copy-done.3), channel_id=1, source_target_pairs={{0,1},{1,0},{2,3},{3,2},{4,5},{5,4},{6,7},{7,6},{8,9},{9,8},{10,11... | collective-permute-start | bytes 2457608 | tf_op jit(solution)/shard_map/ppermute | solution.py:266
  51.2 17.2 %collective-permute-start.9 = (bf16[320,1280]{1,0:T(8,128)(2,1)}, bf16[320,1280]{1,0:T(8,128)(2,1)}, u32[]{:S(2)}, u32[]{:S(2)}) collective-permute-start(bf16[320,1280]{1,0:T(8,128)(2,1)} %collective-permute-done.8.rest_2_), channel_id=1, source_target_pairs={{0,1},{1,0},{2,3},{3,2},{4,5},{5,4},{6,7},{7,6},{8,9},{9,8},{10,11... | collective-permute-start | bytes 2457608 | tf_op jit(solution)/shard_map/ppermute | solution.py:266
  51.7 2.9 %collective-permute-start.2 = (bf16[16,4,1536]{2,1,0:T(4,128)(2,1)S(1)}, bf16[16,4,1536]{2,1,0:T(4,128)(2,1)S(1)}, u32[]{:S(2)}, u32[]{:S(2)}) collective-permute-start(bf16[16,4,1536]{2,1,0:T(4,128)(2,1)S(1)} %all-to-all-done.1.here), channel_id=1, source_target_pairs={{0,1},{1,0},{2,3},{3,2},{4,5},{5,4},{6,7},{7,6},{8,9},{9,8},{10,11... | collective-permute-start | bytes 589832 | tf_op jit(solution)/shard_map/ppermute | solution.py:266
  54.5 7.4 %collective-permute-start.3 = (bf16[16,4,1536]{2,1,0:T(4,128)(2,1)S(1)}, bf16[16,4,1536]{2,1,0:T(4,128)(2,1)}, u32[]{:S(2)}, u32[]{:S(2)}) collective-permute-start(bf16[16,4,1536]{2,1,0:T(4,128)(2,1)S(1)} %all-to-all-done.1.here), channel_id=1, source_target_pairs={{1,2},{2,1},{5,6},{6,5},{9,10},{10,9},{13,14},{14,13},{17,18},{18,... | collective-permute-start | bytes 589832 | tf_op jit(solution)/shard_map/ppermute | solution.py:269
  58.7 5.1 %copy-start = (bf16[12,2,8,1280]{3,2,1,0:T(8,128)(2,1)S(1)}, bf16[12,2,8,1280]{3,2,1,0:T(8,128)(2,1)}, u32[]{:S(2)}) copy-start(bf16[12,2,8,1280]{3,2,1,0:T(8,128)(2,1)} %param.12) | copy-start | bytes 1474564

commit v2 on v1

v2 whole, which is shorter than its diff:
```python
import functools

import jax
import jax.numpy as jnp
from jax import lax
from jax.experimental import pallas as pl
from jax.experimental.pallas import tpu as pltpu
from jax.sharding import PartitionSpec as P

EPSILON = 1e-06
BF16 = jnp.bfloat16
F32 = jnp.float32
SMEM = pl.BlockSpec(memory_space=pltpu.SMEM)
VMEM = pl.BlockSpec(memory_space=pltpu.VMEM)
ANY = pl.BlockSpec(memory_space=pl.ANY)
VMEM_BYTES = 24 * 1024 * 1024
ALL_BYTES = 60 * 1024 * 1024


def params(vmem_bytes=VMEM_BYTES):
    return pltpu.CompilerParams(vmem_limit_bytes=vmem_bytes)


def split_dot(matrix, values):
    rows = matrix.shape[0]
    high = matrix.astype(BF16)
    low = (matrix - high.astype(F32)).astype(BF16)
    both = jnp.concatenate([high, low], axis=0)
    product = jnp.dot(both, values, preferred_element_type=F32)
    return product[:rows] + product[rows:]


def own_rows(list_ref, rank, per_device, image_dev, capacity):
    first = rank * per_device
    owners = [lax.div(list_ref[first + i], image_dev) for i in range(per_device)]
    rows = []
    for i in range(per_device):
        position = jnp.int32(0)
        for j in range(i):
            position = position + jnp.where(owners[j] == owners[i], 1, 0)
        rows.append(owners[i] * capacity + position)
    return rows


def arrived_rows(list_ref, rank, slots, per_device, image_dev, capacity, row_of):
    for k in range(image_dev):
        row_of[k] = -1

    def source(peer, _):
        def slot(i, seen):
            image = list_ref[peer * per_device + i]
            mine = lax.div(image, image_dev) == rank

            @pl.when(mine)
            def _():
                row_of[image - rank * image_dev] = peer * capacity + seen

            return seen + jnp.where(mine, 1, 0)

        lax.fori_loop(0, per_device, slot, jnp.int32(0), unroll=True)
        return 0

    lax.fori_loop(0, slots // per_device, source, 0)


def pre_kernel(dims, start, row_weight, col_weight, sam_feats, own, core_part, edge_part):
    per_device, grid_rows = dims
    sp = lax.axis_index("sp")
    even = lax.rem(sp, 2) == 0
    up, down = 2 * sp - 1, 2 * sp + 2
    targets = [2 * sp, 2 * sp + 1, jnp.where(even, down, up), jnp.where(even, up, down)]
    col_count = col_weight.shape[1]
    across = jnp.concatenate([col_weight[...]] * 4, axis=1)
    column_row = lax.broadcasted_iota(jnp.int32, across.shape, 1) // col_count
    blocks = []
    for y in targets:
        inside = jnp.logical_and(y >= 0, y < grid_rows)
        line = jnp.clip(y, 0, grid_rows - 1)
        first_row = start[line] - 4 * sp
        taps = jnp.zeros(across.shape, F32)
        for tap in range(row_weight.shape[0]):
            weight = jnp.where(inside, row_weight[tap, line], 0.0)
            taps = taps + jnp.where(column_row == first_row + tap, weight, 0.0)
        blocks.append(across * taps)
    matrix = jnp.concatenate(blocks, axis=0)
    wide = own.shape[1]
    half = wide // 2
    for i in range(per_device):
        result = split_dot(matrix, sam_feats[i])
        own[i] = result[:wide]
        core_part[i] = result[wide : wide + half].astype(BF16)
        edge_part[i] = result[wide + half :].astype(BF16)


def pack_kernel(
    dims, dino_list, sam_list, dino_feats, own, core_part, edge_part, packed
):
    per_device, image_dev, capacity = dims
    rank = lax.axis_index("img")
    even = lax.rem(lax.axis_index("sp"), 2) == 0
    half, sam_width = core_part.shape[1:]
    patch = 2 * half
    sam_blocks = sam_width // 128
    for i, row in enumerate(own_rows(sam_list, rank, per_device, image_dev, capacity)):
        core = core_part[i].astype(F32)
        edge = edge_part[i].astype(F32)
        top = own[i, :half] + jnp.where(even, edge, core)
        bottom = own[i, half:] + jnp.where(even, core, edge)
        values = jnp.concatenate([top, bottom], axis=0).astype(BF16)
        for n in range(sam_blocks):
            packed[row, n * patch : (n + 1) * patch, :] = values[:, n * 128 : (n + 1) * 128]
    first = sam_blocks * patch
    packed[:, first:, :] = jnp.zeros((packed.shape[0], packed.shape[1] - first, 128), BF16)
    for i, row in enumerate(own_rows(dino_list, rank, per_device, image_dev, capacity)):
        values = dino_feats[i].astype(F32)
        blocks = [values[:, n * 128 : (n + 1) * 128] for n in range(values.shape[1] // 128)]
        packed[row, first:, :] = jnp.concatenate(blocks, axis=0).astype(BF16)


def select_kernel(dims, dino_list, arrived, chosen, row_of):
    slots, per_device, image_dev, capacity = dims
    rank = lax.axis_index("img")
    arrived_rows(dino_list, rank, slots, per_device, image_dev, capacity, row_of)
    first = arrived.shape[1] - chosen.shape[1]
    for k in range(image_dev):
        row = row_of[k]
        values = arrived[jnp.maximum(row, 0), first:, :]
        chosen[k] = jnp.where(row >= 0, values, jnp.zeros_like(values))


def target_kernel(row_weight, col_weight, here, core_side, edge_side, target, stacked):
    sp = lax.axis_index("sp")
    even = lax.rem(sp, 2) == 0
    images, blocks = here.shape[0], here.shape[1] // 8
    cols = col_weight.shape[1]
    core = core_side[...].astype(F32)
    edge = edge_side[...].astype(F32)
    above = jnp.where(even, edge, core)
    below = jnp.where(even, core, edge)
    for k, values in enumerate((above, here[...].astype(F32), below)):
        for n in range(blocks):
            part = values[:, 8 * n : 8 * n + 8, :].reshape(images * 8, 128)
            stacked[k * images * 8 : (k + 1) * images * 8, n * 128 : (n + 1) * 128] = part.astype(BF16)
    patch_cols = col_weight.shape[0]
    shape = (patch_cols, 3 * images * 8)
    column = lax.broadcasted_iota(jnp.int32, shape, 1)
    tap_of = column // (images * 8)
    image_of = (column // 8) % images
    block_of = (column // cols) % 2
    j_of = column % cols
    across = jnp.zeros(shape, F32)
    for j in range(cols):
        across = across + jnp.where(j_of == j, col_weight[:, j : j + 1], 0.0)
    lines = []
    for y in range(2):
        taps = jnp.zeros(shape, F32)
        for k in range(3):
            taps = taps + jnp.where(tap_of == k, row_weight[k, 2 * sp + y], 0.0)
        lines.append(across * taps)
    base = jnp.concatenate(lines, axis=0)
    image_of = jnp.concatenate([image_of] * 2, axis=0)
    block_of = jnp.concatenate([block_of] * 2, axis=0)
    matrix = jnp.concatenate(
        [
            jnp.where(jnp.logical_and(image_of == k, block_of == side), base, 0.0)
            for side in range(2)
            for k in range(images)
        ],
        axis=0,
    )
    result = split_dot(matrix, stacked[...]).astype(BF16)
    rows = target.shape[0]
    for n in range(blocks):
        for side in range(2):
            at = (2 * n + side) * 128
            target[:, at : at + 128] = result[side * rows : (side + 1) * rows, n * 128 : (n + 1) * 128]


def load_whole(pieces, by_neighbour, whole, sems, first_sem):
    rows = pieces[0].shape[0]
    places = [(pieces[0], 0)]
    if len(pieces) > 1:
        sp = lax.axis_index("sp")
        here, core = sp // 2 * 2, lax.rem(sp, 2)
        first = lax.rem(lax.axis_index("img"), 2) * (rows // 2) if by_neighbour else 0
        places = [(pieces[0], (here + core) * rows), (pieces[1], (here + 1 - core) * rows)]
        for far, at in ((2 - here + core, 2), (3 - here - core, 4)):
            places.append((pieces[at], far * rows + first))
            places.append((pieces[at + 1], far * rows + rows // 2 - first))
    copies = []
    for n, (piece, offset) in enumerate(places):
        place = pl.ds(pl.multiple_of(offset, 16), piece.shape[0])
        copies.append(pltpu.make_async_copy(piece, whole.at[place, :], sems.at[first_sem + n]))
    for copy in copies:
        copy.start()
    return copies


def row_sum(values):
    return jnp.sum(values, axis=-1, keepdims=True)


def sam_kernel(
    counts, dims, sam_list, student, arrived, *rest
):
    slots, per_device, image_dev, capacity = dims
    sam_pieces, dino_pieces = rest[: counts[0]], rest[counts[0] : sum(counts)]
    grad, predicted, dino_whole, rows_in, packs_in, sam_whole, delta, row_of, sems = rest[sum(counts) :]
    rows_copy = pltpu.make_async_copy(student, rows_in, sems.at[0])
    packs_copy = pltpu.make_async_copy(arrived, packs_in, sems.at[1])
    rows_copy.start()
    sam_copies = load_whole(sam_pieces, True, sam_whole, sems, 2)
    packs_copy.start()
    dino_copies = load_whole(dino_pieces, False, dino_whole, sems, 2 + counts[0])
    rank = lax.axis_index("img")
    arrived_rows(sam_list, rank, slots, per_device, image_dev, capacity, row_of)
    for copy in (rows_copy, *sam_copies):
        copy.wait()
    sam_predicted = jnp.dot(rows_in[...], sam_whole[...], preferred_element_type=F32)
    packs_copy.wait()
    patch = rows_in.shape[0] // image_dev
    for k in range(image_dev):
        row = row_of[k]
        at = jnp.maximum(row, 0)
        rows = slice(k * patch, (k + 1) * patch)
        for n in range(sam_whole.shape[1] // 128):
            columns = slice(n * 128, (n + 1) * 128)
            target = packs_in[at, n * patch : (n + 1) * patch, :].astype(F32)
            error = jnp.clip(sam_predicted[rows, columns] - target, -1.0, 1.0)
            delta[rows, columns] = jnp.where(row >= 0, error, 0.0).astype(BF16)
    grad[...] = lax.dot_general(
        delta[...], sam_whole[...], (((1,), (1,)), ((), ())), preferred_element_type=F32
    ).astype(BF16)
    for copy in dino_copies:
        copy.wait()
    predicted[...] = jnp.dot(rows_in[...], dino_whole[...], preferred_element_type=F32)


def dino_kernel(predicted, target, sam_grad, whole, out, delta):
    p = predicted[...]
    t = target[...].astype(F32)
    pred_inv = 1.0 / jnp.sqrt(row_sum(p * p) + EPSILON)
    goal_inv = 1.0 / jnp.sqrt(row_sum(t * t) + EPSILON)
    cosine = row_sum(p * t) * pred_inv * goal_inv
    features = p.shape[-1]
    delta[...] = (
        (features * pred_inv) * ((cosine * pred_inv) * p - goal_inv * t)
    ).astype(BF16)
    back = lax.dot_general(
        delta[...], whole[...], (((1,), (1,)), ((), ())), preferred_element_type=F32
    )
    total = back.astype(BF16).astype(F32) + sam_grad[...].astype(F32)
    out[...] = total.astype(BF16)


def after(first, *rest):
    return lax.optimization_barrier((first, *rest))


def pair_perms(count):
    core = [(i, i ^ 1) for i in range(count)]
    edge = []
    for i in range(1, count - 1, 2):
        edge += [(i, i + 1), (i + 1, i)]
    return core, edge


def shards(
    student,
    dino_feats,
    sam_feats,
    dino_proj,
    sam_proj,
    dino_list,
    sam_list,
    dino_row_weight,
    dino_col_weight,
    sam_start,
    sam_row_weight,
    sam_col_weight,
):
    peers = lax.axis_size("img")
    sp_count = lax.axis_size("sp")
    images, rows_dev, patch_cols, width = student.shape
    slots = dino_list.shape[0]
    per_device = slots // peers
    capacity = (2 * per_device + peers - 1) // peers
    buffer_rows = peers * capacity
    patch = rows_dev * patch_cols
    grid_rows = dino_row_weight.shape[0]
    dino_cols, dino_width = dino_feats.shape[2:]
    sam_rows, sam_cols, sam_width = sam_feats.shape[1:]
    core_perm, edge_perm = pair_perms(sp_count)

    def core_swap(values):
        return lax.ppermute(values, "sp", core_perm)

    def edge_swap(values):
        return lax.ppermute(values, "sp", edge_perm)

    dims = (per_device, images, capacity)
    shared = sp_count == 4 and peers % 2 == 0
    pack_rows = patch * sam_width // 128 + dino_cols * dino_width // 128
    half_shape = jax.ShapeDtypeStruct((per_device, patch_cols, sam_width), BF16)
    own, core_part, edge_part = pl.pallas_call(
        functools.partial(pre_kernel, (per_device, grid_rows)),
        out_shape=(
            jax.ShapeDtypeStruct((per_device, patch, sam_width), F32),
            half_shape,
            half_shape,
        ),
        in_specs=[SMEM] * 2 + [VMEM] * 2,
        out_specs=(VMEM,) * 3,
        compiler_params=params(ALL_BYTES),
        name="pre",
    )(
        sam_start,
        sam_row_weight.T,
        sam_col_weight,
        sam_feats.reshape(per_device, sam_rows * sam_cols, sam_width),
    )
    edge_got = edge_swap(edge_part)
    core_got = core_swap(core_part)
    packed = pl.pallas_call(
        functools.partial(pack_kernel, dims),
        out_shape=jax.ShapeDtypeStruct((buffer_rows, pack_rows, 128), BF16),
        in_specs=[SMEM] * 2 + [VMEM] * 4,
        out_specs=VMEM,
        compiler_params=params(ALL_BYTES),
        name="pack",
    )(
        dino_list,
        sam_list,
        dino_feats.reshape(per_device, dino_cols, dino_width),
        own,
        core_got,
        edge_got,
    )

    arrived = lax.all_to_all(packed, "img", split_axis=0, concat_axis=0, tiled=True)

    if shared:
        chip_perm = [(i, i ^ 2) for i in range(4)]
        near_perm = [(i, i ^ 1) for i in range(peers)]
        half = sam_proj.shape[0] // 2
        near = lax.dynamic_slice_in_dim(sam_proj, lax.axis_index("img") % 2 * half, half, 0)
        _, _, near = after(edge_got, core_got, near)
        sam_far = [lax.ppermute(near, "sp", chip_perm)]
        sam_far[0], _, dino_shard = after(sam_far[0], packed, dino_proj)
        sam_far.append(lax.ppermute(sam_far[0], "img", near_perm))
        dino_far = [
            lax.ppermute(part, "sp", chip_perm) for part in (dino_shard[:half], dino_shard[half:])
        ]
        dino_pieces = [dino_proj, core_swap(dino_proj), *dino_far, *map(core_swap, dino_far)]
        sam_pieces = [sam_proj, core_swap(sam_proj), *sam_far, *map(core_swap, sam_far)]
    else:
        dino_pieces = [lax.all_gather(dino_proj, "sp", axis=0, tiled=True)]
        sam_pieces = [lax.all_gather(sam_proj, "sp", axis=0, tiled=True)]

    dino_rows = dino_cols * dino_width // 128
    chosen = pl.pallas_call(
        functools.partial(select_kernel, (slots, *dims)),
        out_shape=jax.ShapeDtypeStruct((images, dino_rows, 128), BF16),
        in_specs=[SMEM, VMEM],
        out_specs=VMEM,
        scratch_shapes=[pltpu.SMEM((images,), jnp.int32)],
        compiler_params=params(),
        name="select",
    )(dino_list, arrived)
    target = pl.pallas_call(
        target_kernel,
        out_shape=jax.ShapeDtypeStruct((images * patch, dino_width), BF16),
        in_specs=[SMEM] + [VMEM] * 4,
        out_specs=VMEM,
        scratch_shapes=[pltpu.VMEM((3 * images * 8, dino_width // 2), BF16)],
        compiler_params=params(),
        name="target",
    )(dino_row_weight.T, dino_col_weight, chosen, core_swap(chosen), edge_swap(chosen))

    rows = student.reshape(images * patch, width)
    counts = (len(sam_pieces), len(dino_pieces))
    sam_grad, dino_predicted, dino_whole = pl.pallas_call(
        functools.partial(sam_kernel, counts, (slots, *dims)),
        out_shape=(
            jax.ShapeDtypeStruct(rows.shape, BF16),
            jax.ShapeDtypeStruct((rows.shape[0], dino_width), F32),
            jax.ShapeDtypeStruct((width, dino_width), BF16),
        ),
        in_specs=[SMEM] + [ANY] * (2 + sum(counts)),
        out_specs=(VMEM,) * 3,
        scratch_shapes=[
            pltpu.VMEM(rows.shape, BF16),
            pltpu.VMEM(arrived.shape, BF16),
            pltpu.VMEM((width, sam_width), BF16),
            pltpu.VMEM((rows.shape[0], sam_width), BF16),
            pltpu.SMEM((images,), jnp.int32),
            pltpu.SemaphoreType.DMA((2 + sum(counts),)),
        ],
        compiler_params=params(),
        name="sam",
    )(sam_list, rows, arrived, *sam_pieces, *dino_pieces)
    out = pl.pallas_call(
        dino_kernel,
        out_shape=jax.ShapeDtypeStruct(rows.shape, BF16),
        in_specs=[VMEM] * 4,
        out_specs=VMEM,
        scratch_shapes=[pltpu.VMEM((rows.shape[0], dino_width), BF16)],
        compiler_params=params(),
        name="dino",
    )(dino_predicted, target, sam_grad, dino_whole)
    return out.reshape(student.shape)


def solution(mesh):
    placed = (
        P("img", "sp", None, None),
        P("img", "sp", None, None),
        P("img", "sp", None, None),
        P("sp", None),
        P("sp", None),
        P(),
        P(),
        P(),
        P(),
        P(),
        P(),
        P(),
    )
    return jax.shard_map(
        shards, mesh=mesh, in_specs=placed, out_specs=P("img", "sp", None, None), check_vma=False
    )
```

time: 74.1 us -> 61.8 us (0.83)
  waiting for transfers between devices: 31.9 us -> 16.3 us
  Pallas kernels: 14.4 us -> 16.7 us
  starting transfers between devices: 23.4 us -> 24.4 us
    ppermute x2, waiting for transfers between devices: 29.1 us -> 0.96 us  [edge_swap(): return lax.ppermute(values, 'sp', edge_perm)]
    ppermute x2 -> x4, waiting for transfers between devices: 0.01 us -> 15.3 us  [the longest x2 14.3 us: shards(): lax.ppermute(part, 'sp', chip_perm)]
    ppermute x6 -> x8, starting transfers between devices: 2.67 us -> 8.14 us  [core_swap(): return lax.ppermute(values, 'sp', core_perm)]
    all_to_all x2 -> x1, starting transfers between devices: 11.6 us -> 6.13 us  [shards(): lax.all_to_all(packed, 'img', split_axis=0, concat_axis=0, tiled=True)]
    ppermute x6 -> x8, waiting for transfers between devices: 2.8 us -> 0.02 us  [core_swap(): return lax.ppermute(values, 'sp', core_perm)]
    pallas_call x5 -> x6, Pallas kernels: 14.4 us -> 16.7 us  [the longest x1 5.89 us: shards(): pl.pallas_call(functools.partial(sam_kernel, counts, (slots, *dims)), out...]
    unnamed x25 -> x19, local copies, waits for them, and re-layouts: 3.71 us -> 1.77 us
    dynamic_slice x0 -> x1, local copies, waits for them, and re-layouts: none -> 1.78 us  [shards(): lax.dynamic_slice_in_dim(sam_proj, lax.axis_index('img') % 2 * half, half...]
  transfers between devices with their start and end apart: 12 -> 15, of which waited for: 3 -> 4; matrix products, arithmetic and copies ran while one was open for 1% -> 3% of each run, Pallas kernels for 13% -> 16%
where the time goes in v2:
time: 61.8 us; the launch traced here: 61.2 us
  starting transfers between devices  24.4 us (39%)
  Pallas kernels  16.7 us (27%)
  waiting for transfers between devices  16.3 us (26%)
  local copies, waits for them, and re-layouts  3.61 us (6%)
    ppermute x2, waiting for transfers between devices, shards(): lax.ppermute(part, 'sp', chip_perm)  14.3 us
    ppermute x8, starting transfers between devices, core_swap(): return lax.ppermute(values, 'sp', core_perm)  8.14 us
    ppermute x2, starting transfers between devices, edge_swap(): return lax.ppermute(values, 'sp', edge_perm)  6.39 us
    all_to_all x1, starting transfers between devices, shards(): lax.all_to_all(packed, 'img', split_axis=0, concat_axis=0, tiled=True)  6.13 us
    pallas_call x1, Pallas kernels, shards(): pl.pallas_call(functools.partial(sam_kernel, counts, (slots, *dims)), out...  5.89 us
    pallas_call x1, Pallas kernels, shards(): pl.pallas_call(functools.partial(pre_kernel, (per_device, grid_rows)), ou...  2.67 us
    pallas_call x1, Pallas kernels, shards(): pl.pallas_call(dino_kernel, out_shape=jax.ShapeDtypeStruct(rows.shape, BF...  2.59 us
    ppermute x1, starting transfers between devices, shards(): sam_far.append(lax.ppermute(sam_far[0], 'img', near_perm))  2.24 us
  transfers between devices with their start and end apart: 15, of which 4 were waited for; matrix products, arithmetic and copies ran while one was open for 3% of the time, Pallas kernels for 16%

profile of v2, /device:TPU:1, one launch (start us, length us, event | category | flops | bytes accessed | tf_op | source)
XLA Modules:
  0.0 61.2 jit_solution(11013652886817283101)
XLA Ops:
  0.0 0.0 copy-start.5
  0.0 2.7 %pre.1 = (f32[6,16,1280]{2,1,0:T(8,128)}, bf16[6,8,1280]{2,1,0:T(8,128)(2,1)}, bf16[6,8,1280]{2,1,0:T(8,128)(2,1)}) custom-call(s32[8]{0:T(128)} %start.1, f32[4,8]{1,0:T(4,128)} %bitcast.10, f32[8,16]{1,0:T(8,128)} %col_weight.2, bf16[6,64,1280]{2,1,0:T(8,128)(2,1)} %bitcast.8), custom_call_target="tpu_custom_call" | custom-call | tf_op jit(solution)/shard_map/pre/pallas_call | solution.py:305
  2.7 0.0 collective-permute-start
  2.8 4.5 %collective-permute-start.1 = (bf16[6,8,1280]{2,1,0:T(8,128)(2,1)}, bf16[6,8,1280]{2,1,0:T(8,128)(2,1)S(1)}, u32[]{:S(2)}, u32[]{:S(2)}) collective-permute-start(bf16[6,8,1280]{2,1,0:T(8,128)(2,1)} %get-tuple-element.16), channel_id=1, source_target_pairs={{1,2},{2,1},{5,6},{6,5},{9,10},{10,9},{13,14},{14,13},{17,18},{18,... | collective-permute-start | bytes 368648 | tf_op jit(solution)/shard_map/ppermute | solution.py:299
  7.3 1.8 %constant_dynamic-slice_fusion = bf16[160,1280]{1,0:T(8,128)(2,1)} fusion(bf16[320,1280]{1,0:T(8,128)(2,1)} %rest_0_.1, s32[]{:T(128)S(6)} %select_n.11), kind=kLoop, calls=%fused_computation | loop fusion | bytes 819204 | tf_op jit(solution)/shard_map/dynamic_slice | solution.py:346
  9.0 1.0 %collective-permute-done.1.edge_part = bf16[6,8,1280]{2,1,0:T(8,128)(2,1)S(1)} collective-permute-done((bf16[6,8,1280]{2,1,0:T(8,128)(2,1)}, bf16[6,8,1280]{2,1,0:T(8,128)(2,1)S(1)}, u32[]{:S(2)}, u32[]{:S(2)}) %collective-permute-start.1) | collective-permute-done | bytes 122912 | tf_op jit(solution)/shard_map/ppermute | solution.py:299
  10.0 0.0 collective-permute-start.3
  10.0 0.6 %copy-done.7 = bf16[6,8,1280]{2,1,0:T(8,128)(2,1)} copy-done((bf16[6,8,1280]{2,1,0:T(8,128)(2,1)}, bf16[6,8,1280]{2,1,0:T(8,128)(2,1)S(1)}, u32[]{:S(2)}) %copy-start.7) | copy-done | bytes 122904
  10.6 2.2 %pack.1 = bf16[16,208,128]{2,1,0:T(8,128)(2,1)} custom-call(s32[48]{0:T(128)} %dino_list.3, s32[48]{0:T(128)} %sam_list.3, bf16[6,4,1536]{2,1,0:T(4,128)(2,1)} %bitcast.9, f32[6,16,1280]{2,1,0:T(8,128)} %get-tuple-element.14.own, bf16[6,8,1280]{2,1,0:T(8,128)(2,1)} %copy-done.6, bf16[6,8,1280]{2,1,0:T(8,128)(2,1)} %copy-done.7), custom_call_target="tpu_custom_call" | custom-call | tf_op jit(solution)/shard_map/pack/pallas_call | solution.py:324
  12.8 6.1 %all-to-all-start = ((bf16[16,208,128]{2,1,0:T(8,128)(2,1)}), bf16[16,208,128]{2,1,0:T(8,128)(2,1)S(1)}, u32[]{:S(2)}, u32[]{:S(2)}) async-start(bf16[16,208,128]{2,1,0:T(8,128)(2,1)} %pack.1), calls=%async_computation | async-start | bytes 1703936 | tf_op jit(solution)/shard_map/all_to_all | solution.py:340
  19.0 1.2 %collective-permute-start.2 = (bf16[320,1280]{1,0:T(8,128)(2,1)S(1)}, bf16[320,1280]{1,0:T(8,128)(2,1)S(1)}, u32[]{:S(2)}, u32[]{:S(2)}) collective-permute-start(bf16[320,1280]{1,0:T(8,128)(2,1)S(1)} %copy-done.1), channel_id=1, source_target_pairs={{0,1},{1,0},{2,3},{3,2},{4,5},{5,4},{6,7},{7,6},{8,9},{9,8},{10,11... | collective-permute-start | bytes 2457608 | tf_op jit(solution)/shard_map/ppermute | solution.py:296
  20.2 0.1 collective-permute-start.7
  20.3 1.0 %collective-permute-done.3.rest_2_ = bf16[160,1280]{1,0:T(8,128)(2,1)} collective-permute-done((bf16[160,1280]{1,0:T(8,128)(2,1)}, bf16[160,1280]{1,0:T(8,128)(2,1)}, u32[]{:S(2)}, u32[]{:S(2)}) %collective-permute-start.3) | collective-permute-done | bytes 409632 | tf_op jit(solution)/shard_map/ppermute | solution.py:348
  21.3 0.1 fusion
  21.4 0.1 collective-permute-start.8
  21.4 1.5 %collective-permute-start.9 = (bf16[160,1536]{1,0:T(8,128)(2,1)S(1)}, bf16[160,1536]{1,0:T(8,128)(2,1)}, u32[]{:S(2)}, u32[]{:S(2)}) collective-permute-start(bf16[160,1536]{1,0:T(8,128)(2,1)S(1)} %get-tuple-element.23), channel_id=1, source_target_pairs={{0,2},{1,3},{2,0},{3,1},{4,6},{5,7},{6,4},{7,5},{8,10},{9,11},{10,... | collective-permute-start | bytes 1474568 | tf_op jit(solution)/shard_map/ppermute | solution.py:352
  22.9 2.2 %collective-permute-start.4 = (bf16[160,1280]{1,0:T(8,128)(2,1)}, bf16[160,1280]{1,0:T(8,128)(2,1)}, u32[]{:S(2)}, u32[]{:S(2)}) collective-permute-start(bf16[160,1280]{1,0:T(8,128)(2,1)} %collective-permute-done.3.rest_2_), channel_id=1, source_target_pairs={{0,4},{4,0},{8,12},{12,8},{16,20},{20,16},{24,28},{28,24},{1,5},{5... | collective-permute-start | bytes 1228808 | tf_op jit(solution)/shard_map/ppermute | solution.py:350
  25.1 1.2 %collective-permute-start.5 = (bf16[160,1280]{1,0:T(8,128)(2,1)}, bf16[160,1280]{1,0:T(8,128)(2,1)}, u32[]{:S(2)}, u32[]{:S(2)}) collective-permute-start(bf16[160,1280]{1,0:T(8,128)(2,1)} %collective-permute-done.3.rest_2_), channel_id=1, source_target_pairs={{0,1},{1,0},{2,3},{3,2},{4,5},{5,4},{6,7},{7,6},{8,9},{9,8},{10,11... | collective-permute-start | bytes 1228808 | tf_op jit(solution)/shard_map/ppermute | solution.py:296
  26.4 7.0 %collective-permute-done.8.rest_8_ = bf16[160,1536]{1,0:T(8,128)(2,1)} collective-permute-done((bf16[160,1536]{1,0:T(8,128)(2,1)S(1)}, bf16[160,1536]{1,0:T(8,128)(2,1)}, u32[]{:S(2)}, u32[]{:S(2)}) %collective-permute-start.8) | collective-permute-done | bytes 491552 | tf_op jit(solution)/shard_map/ppermute | solution.py:352
  33.4 3.2 %collective-permute-start.10 = (bf16[160,1536]{1,0:T(8,128)(2,1)}, bf16[160,1536]{1,0:T(8,128)(2,1)}, u32[]{:S(2)}, u32[]{:S(2)}) collective-permute-start(bf16[160,1536]{1,0:T(8,128)(2,1)} %collective-permute-done.8.rest_8_), channel_id=1, source_target_pairs={{0,1},{1,0},{2,3},{3,2},{4,5},{5,4},{6,7},{7,6},{8,9},{9,8},{10,11... | collective-permute-start | bytes 1474568 | tf_op jit(solution)/shard_map/ppermute | solution.py:296
  36.6 7.3 %collective-permute-done.9.rest_9_ = bf16[160,1536]{1,0:T(8,128)(2,1)} collective-permute-done((bf16[160,1536]{1,0:T(8,128)(2,1)S(1)}, bf16[160,1536]{1,0:T(8,128)(2,1)}, u32[]{:S(2)}, u32[]{:S(2)}) %collective-permute-start.9) | collective-permute-done | bytes 491552 | tf_op jit(solution)/shard_map/ppermute | solution.py:352
  43.9 1.8 %collective-permute-start.11 = (bf16[160,1536]{1,0:T(8,128)(2,1)}, bf16[160,1536]{1,0:T(8,128)(2,1)}, u32[]{:S(2)}, u32[]{:S(2)}) collective-permute-start(bf16[160,1536]{1,0:T(8,128)(2,1)} %collective-permute-done.9.rest_9_), channel_id=1, source_target_pairs={{0,1},{1,0},{2,3},{3,2},{4,5},{5,4},{6,7},{7,6},{8,9},{9,8},{10,11... | collective-permute-start | bytes 1474568 | tf_op jit(solution)/shard_map/ppermute | solution.py:296
  45.7 0.0 collective-permute-start.6
  45.7 1.5 %select.3.here = bf16[12,48,128]{2,1,0:T(8,128)(2,1)} custom-call(s32[48]{0:T(128)S(1)} %copy-done.3, bf16[16,208,128]{2,1,0:T(8,128)(2,1)S(1)} %all-to-all-done.arrived), custom_call_target="tpu_custom_call" | custom-call | tf_op jit(solution)/shard_map/select/pallas_call | solution.py:361
  47.2 0.5 collective-permute-start.12
  47.7 1.9 %collective-permute-start.13 = (bf16[12,48,128]{2,1,0:T(8,128)(2,1)}, bf16[12,48,128]{2,1,0:T(8,128)(2,1)}, u32[]{:S(2)}, u32[]{:S(2)}) collective-permute-start(bf16[12,48,128]{2,1,0:T(8,128)(2,1)} %select.3.here), channel_id=1, source_target_pairs={{1,2},{2,1},{5,6},{6,5},{9,10},{10,9},{13,14},{14,13},{17,18},{18,... | collective-permute-start | bytes 442376 | tf_op jit(solution)/shard_map/ppermute | solution.py:299
  49.7 0.1 copy.13.col_weight
  49.8 0.0 copy-start.2
  49.8 1.0 %copy-done.2 = bf16[12,2,8,1280]{3,2,1,0:T(8,128)(2,1)S(1)} copy-done((bf16[12,2,8,1280]{3,2,1,0:T(8,128)(2,1)S(1)}, bf16[12,2,8,1280]{3,2,1,0:T(8,128)(2,1)}, u32[]{:S(2)}) %copy-start.2) | copy-done | bytes 491544
  50.8 5.9 %sam.1 = (bf16[192,1280]{1,0:T(8,128)(2,1)S(1)}, f32[192,1536]{1,0:T(8,128)S(1)}, bf16[1280,1536]{1,0:T(8,128)(2,1)S(1)}) custom-call(s32[48]{0:T(128)S(1)} %copy-done.5, bf16[192,1280]{1,0:T(8,128)(2,1)S(1)} %bitcast.6, bf16[16,208,128]{2,1,0:T(8,128)(2,1)S(1)} %all-to-all-done.arrived, bf16[320,1280]{1,0:T(8,128)(2,1)S(1)} %copy-done.1, ...), custom_call_target="tpu_custom_call" | custom-call | tf_op jit(solution)/shard_map/sam/pallas_call | solution.py:382
  56.7 1.9 %target.1 = bf16[192,1536]{1,0:T(8,128)(2,1)S(1)} custom-call(f32[3,8]{1,0:T(4,128)S(1)} %bitcast.7, f32[8,4]{1,0:T(8,128)S(1)} %copy.13.col_weight, bf16[12,48,128]{2,1,0:T(8,128)(2,1)} %select.3.here, bf16[12,48,128]{2,1,0:T(8,128)(2,1)} %collective-permute-done.12.core_side, bf16[12,48,128]{2,1,0:T(8,128)(2,1)} %collective-permute-done.13.edge_side), custom_call_target="tpu_custom_call" | custom-call | tf_op jit(solution)/shard_map/target/pallas_call | solution.py:370
  58.6 2.6 %dino.1 = bf16[192,1280]{1,0:T(8,128)(2,1)} custom-call(f32[192,1536]{1,0:T(8,128)S(1)} %get-tuple-element.20.predicted, bf16[192,1536]{1,0:T(8,128)(2,1)S(1)} %target.1, bf16[192,1280]{1,0:T(8,128)(2,1)S(1)} %get-tuple-element.21.sam_grad, bf16[1280,1536]{1,0:T(8,128)(2,1)S(1)} %get-tuple-element.22.whole), custom_call_target="tpu_custom_call" | custom-call | tf_op jit(solution)/shard_map/dino/pallas_call | solution.py:402
  (25 shorter events, 0.1 us)
Async XLA Ops:
  0.0 19.0 %copy-start.1 = (bf16[320,1280]{1,0:T(8,128)(2,1)S(1)}, bf16[320,1280]{1,0:T(8,128)(2,1)}, u32[]{:S(2)}) copy-start(bf16[320,1280]{1,0:T(8,128)(2,1)} %rest_0_.1) | copy-start | bytes 2457604
  0.0 45.7 %copy-start.3 = (s32[48]{0:T(128)S(1)}, s32[48]{0:T(128)}, u32[]{:S(2)}) copy-start(s32[48]{0:T(128)} %dino_list.3) | copy-start | bytes 580
  0.0 20.2 %copy-start = (bf16[320,1536]{1,0:T(8,128)(2,1)S(1)}, bf16[320,1536]{1,0:T(8,128)(2,1)}, u32[]{:S(2)}) copy-start(bf16[320,1536]{1,0:T(8,128)(2,1)} %rest_6_.1) | copy-start | bytes 2949124
  0.0 49.6 %copy-start.8 = (f32[8,4]{0,1:T(4,128)S(1)}, f32[8,4]{0,1:T(4,128)}, u32[]{:S(2)}) copy-start(f32[8,4]{0,1:T(4,128)} %param.20) | copy-start | bytes 388
  0.0 49.7 %copy-start.5 = (s32[48]{0:T(128)S(1)}, s32[48]{0:T(128)}, u32[]{:S(2)}) copy-start(s32[48]{0:T(128)} %sam_list.3) | copy-start | bytes 580
  2.7 6.3 %collective-permute-start = (bf16[6,8,1280]{2,1,0:T(8,128)(2,1)}, bf16[6,8,1280]{2,1,0:T(8,128)(2,1)S(1)}, u32[]{:S(2)}, u32[]{:S(2)}) collective-permute-start(bf16[6,8,1280]{2,1,0:T(8,128)(2,1)} %get-tuple-element.15), channel_id=1, source_target_pairs={{0,1},{1,0},{2,3},{3,2},{4,5},{5,4},{6,7},{7,6},{8,9},{9,8},{10,11... | collective-permute-start | bytes 368648 | tf_op jit(solution)/shard_map/ppermute | solution.py:296
  2.8 7.2 %collective-permute-start.1 = (bf16[6,8,1280]{2,1,0:T(8,128)(2,1)}, bf16[6,8,1280]{2,1,0:T(8,128)(2,1)S(1)}, u32[]{:S(2)}, u32[]{:S(2)}) collective-permute-start(bf16[6,8,1280]{2,1,0:T(8,128)(2,1)} %get-tuple-element.16), channel_id=1, source_target_pairs={{1,2},{2,1},{5,6},{6,5},{9,10},{10,9},{13,14},{14,13},{17,18},{18,... | collective-permute-start | bytes 368648 | tf_op jit(solution)/shard_map/ppermute | solution.py:299
  9.0 1.0 %copy-start.6 = (bf16[6,8,1280]{2,1,0:T(8,128)(2,1)}, bf16[6,8,1280]{2,1,0:T(8,128)(2,1)S(1)}, u32[]{:S(2)}) copy-start(bf16[6,8,1280]{2,1,0:T(8,128)(2,1)S(1)} %collective-permute-done.core_part) | copy-start | bytes 368644
  10.0 0.6 %copy-start.7 = (bf16[6,8,1280]{2,1,0:T(8,128)(2,1)}, bf16[6,8,1280]{2,1,0:T(8,128)(2,1)S(1)}, u32[]{:S(2)}) copy-start(bf16[6,8,1280]{2,1,0:T(8,128)(2,1)S(1)} %collective-permute-done.1.edge_part) | copy-start | bytes 368644
  10.0 11.3 %collective-permute-start.3 = (bf16[160,1280]{1,0:T(8,128)(2,1)}, bf16[160,1280]{1,0:T(8,128)(2,1)}, u32[]{:S(2)}, u32[]{:S(2)}) collective-permute-start(bf16[160,1280]{1,0:T(8,128)(2,1)} %constant_dynamic-slice_fusion), channel_id=1, source_target_pairs={{0,2},{1,3},{2,0},{3,1},{4,6},{5,7},{6,4},{7,5},{8,10},{9,11},{10,... | collective-permute-start | bytes 1228808 | tf_op jit(solution)/shard_map/ppermute | solution.py:348
  12.8 32.9 %all-to-all-start = ((bf16[16,208,128]{2,1,0:T(8,128)(2,1)}), bf16[16,208,128]{2,1,0:T(8,128)(2,1)S(1)}, u32[]{:S(2)}, u32[]{:S(2)}) async-start(bf16[16,208,128]{2,1,0:T(8,128)(2,1)} %pack.1), calls=%async_computation | async-start | bytes 1703936 | tf_op jit(solution)/shard_map/all_to_all | solution.py:340
  19.0 6.2 %collective-permute-start.2 = (bf16[320,1280]{1,0:T(8,128)(2,1)S(1)}, bf16[320,1280]{1,0:T(8,128)(2,1)S(1)}, u32[]{:S(2)}, u32[]{:S(2)}) collective-permute-start(bf16[320,1280]{1,0:T(8,128)(2,1)S(1)} %copy-done.1), channel_id=1, source_target_pairs={{0,1},{1,0},{2,3},{3,2},{4,5},{5,4},{6,7},{7,6},{8,9},{9,8},{10,11... | collective-permute-start | bytes 2457608 | tf_op jit(solution)/shard_map/ppermute | solution.py:296
  20.2 27.5 %collective-permute-start.7 = (bf16[320,1536]{1,0:T(8,128)(2,1)S(1)}, bf16[320,1536]{1,0:T(8,128)(2,1)}, u32[]{:S(2)}, u32[]{:S(2)}) collective-permute-start(bf16[320,1536]{1,0:T(8,128)(2,1)S(1)} %copy-done), channel_id=1, source_target_pairs={{0,1},{1,0},{2,3},{3,2},{4,5},{5,4},{6,7},{7,6},{8,9},{9,8},{10,11... | collective-permute-start | bytes 2949128 | tf_op jit(solution)/shard_map/ppermute | solution.py:296
  21.4 12.0 %collective-permute-start.8 = (bf16[160,1536]{1,0:T(8,128)(2,1)S(1)}, bf16[160,1536]{1,0:T(8,128)(2,1)}, u32[]{:S(2)}, u32[]{:S(2)}) collective-permute-start(bf16[160,1536]{1,0:T(8,128)(2,1)S(1)} %get-tuple-element.24), channel_id=1, source_target_pairs={{0,2},{1,3},{2,0},{3,1},{4,6},{5,7},{6,4},{7,5},{8,10},{9,11},{10,... | collective-permute-start | bytes 1474568 | tf_op jit(solution)/shard_map/ppermute | solution.py:352
  21.4 22.4 %collective-permute-start.9 = (bf16[160,1536]{1,0:T(8,128)(2,1)S(1)}, bf16[160,1536]{1,0:T(8,128)(2,1)}, u32[]{:S(2)}, u32[]{:S(2)}) collective-permute-start(bf16[160,1536]{1,0:T(8,128)(2,1)S(1)} %get-tuple-element.23), channel_id=1, source_target_pairs={{0,2},{1,3},{2,0},{3,1},{4,6},{5,7},{6,4},{7,5},{8,10},{9,11},{10,... | collective-permute-start | bytes 1474568 | tf_op jit(solution)/shard_map/ppermute | solution.py:352
  22.9 22.8 %collective-permute-start.4 = (bf16[160,1280]{1,0:T(8,128)(2,1)}, bf16[160,1280]{1,0:T(8,128)(2,1)}, u32[]{:S(2)}, u32[]{:S(2)}) collective-permute-start(bf16[160,1280]{1,0:T(8,128)(2,1)} %collective-permute-done.3.rest_2_), channel_id=1, source_target_pairs={{0,4},{4,0},{8,12},{12,8},{16,20},{20,16},{24,28},{28,24},{1,5},{5... | collective-permute-start | bytes 1228808 | tf_op jit(solution)/shard_map/ppermute | solution.py:350
  25.1 22.1 %collective-permute-start.5 = (bf16[160,1280]{1,0:T(8,128)(2,1)}, bf16[160,1280]{1,0:T(8,128)(2,1)}, u32[]{:S(2)}, u32[]{:S(2)}) collective-permute-start(bf16[160,1280]{1,0:T(8,128)(2,1)} %collective-permute-done.3.rest_2_), channel_id=1, source_target_pairs={{0,1},{1,0},{2,3},{3,2},{4,5},{5,4},{6,7},{7,6},{8,9},{9,8},{10,11... | collective-permute-start | bytes 1228808 | tf_op jit(solution)/shard_map/ppermute | solution.py:296
  33.4 16.4 %collective-permute-start.10 = (bf16[160,1536]{1,0:T(8,128)(2,1)}, bf16[160,1536]{1,0:T(8,128)(2,1)}, u32[]{:S(2)}, u32[]{:S(2)}) collective-permute-start(bf16[160,1536]{1,0:T(8,128)(2,1)} %collective-permute-done.8.rest_8_), channel_id=1, source_target_pairs={{0,1},{1,0},{2,3},{3,2},{4,5},{5,4},{6,7},{7,6},{8,9},{9,8},{10,11... | collective-permute-start | bytes 1474568 | tf_op jit(solution)/shard_map/ppermute | solution.py:296
  43.9 5.9 %collective-permute-start.11 = (bf16[160,1536]{1,0:T(8,128)(2,1)}, bf16[160,1536]{1,0:T(8,128)(2,1)}, u32[]{:S(2)}, u32[]{:S(2)}) collective-permute-start(bf16[160,1536]{1,0:T(8,128)(2,1)} %collective-permute-done.9.rest_9_), channel_id=1, source_target_pairs={{0,1},{1,0},{2,3},{3,2},{4,5},{5,4},{6,7},{7,6},{8,9},{9,8},{10,11... | collective-permute-start | bytes 1474568 | tf_op jit(solution)/shard_map/ppermute | solution.py:296
  45.7 4.0 %collective-permute-start.6 = (bf16[160,1280]{1,0:T(8,128)(2,1)}, bf16[160,1280]{1,0:T(8,128)(2,1)}, u32[]{:S(2)}, u32[]{:S(2)}) collective-permute-start(bf16[160,1280]{1,0:T(8,128)(2,1)} %collective-permute-done.4.rest_3_), channel_id=1, source_target_pairs={{0,1},{1,0},{2,3},{3,2},{4,5},{5,4},{6,7},{7,6},{8,9},{9,8},{10,11... | collective-permute-start | bytes 1228808 | tf_op jit(solution)/shard_map/ppermute | solution.py:296
  47.2 9.5 %collective-permute-start.12 = (bf16[12,48,128]{2,1,0:T(8,128)(2,1)}, bf16[12,48,128]{2,1,0:T(8,128)(2,1)}, u32[]{:S(2)}, u32[]{:S(2)}) collective-permute-start(bf16[12,48,128]{2,1,0:T(8,128)(2,1)} %select.3.here), channel_id=1, source_target_pairs={{0,1},{1,0},{2,3},{3,2},{4,5},{5,4},{6,7},{7,6},{8,9},{9,8},{10,11... | collective-permute-start | bytes 442376 | tf_op jit(solution)/shard_map/ppermute | solution.py:296
  47.7 9.0 %collective-permute-start.13 = (bf16[12,48,128]{2,1,0:T(8,128)(2,1)}, bf16[12,48,128]{2,1,0:T(8,128)(2,1)}, u32[]{:S(2)}, u32[]{:S(2)}) collective-permute-start(bf16[12,48,128]{2,1,0:T(8,128)(2,1)} %select.3.here), channel_id=1, source_target_pairs={{1,2},{2,1},{5,6},{6,5},{9,10},{10,9},{13,14},{14,13},{17,18},{18,... | collective-permute-start | bytes 442376 | tf_op jit(solution)/shard_map/ppermute | solution.py:299
  49.8 1.0 %copy-start.2 = (bf16[12,2,8,1280]{3,2,1,0:T(8,128)(2,1)S(1)}, bf16[12,2,8,1280]{3,2,1,0:T(8,128)(2,1)}, u32[]{:S(2)}) copy-start(bf16[12,2,8,1280]{3,2,1,0:T(8,128)(2,1)} %param.12) | copy-start | bytes 1474564
  50.8 5.9 %copy-start.4 = (f32[8,3]{0,1:T(4,128)S(1)}, f32[8,3]{0,1:T(4,128)}, u32[]{:S(2)}) copy-start(f32[8,3]{0,1:T(4,128)} %param.19) | copy-start | bytes 292

commit v3 on v2

--- a/solution.py
+++ b/solution.py
@@ -117,35 +117,15 @@
         packed[row, first:, :] = jnp.concatenate(blocks, axis=0).astype(BF16)
 
 
-def select_kernel(dims, dino_list, arrived, chosen, row_of):
-    slots, per_device, image_dev, capacity = dims
-    rank = lax.axis_index("img")
-    arrived_rows(dino_list, rank, slots, per_device, image_dev, capacity, row_of)
-    first = arrived.shape[1] - chosen.shape[1]
-    for k in range(image_dev):
-        row = row_of[k]
-        values = arrived[jnp.maximum(row, 0), first:, :]
-        chosen[k] = jnp.where(row >= 0, values, jnp.zeros_like(values))
-
-
-def target_kernel(row_weight, col_weight, here, core_side, edge_side, target, stacked):
+def tables_kernel(
+    image_dev, row_weight, col_weight, student, matrix
+):
     sp = lax.axis_index("sp")
-    even = lax.rem(sp, 2) == 0
-    images, blocks = here.shape[0], here.shape[1] // 8
-    cols = col_weight.shape[1]
-    core = core_side[...].astype(F32)
-    edge = edge_side[...].astype(F32)
-    above = jnp.where(even, edge, core)
-    below = jnp.where(even, core, edge)
-    for k, values in enumerate((above, here[...].astype(F32), below)):
-        for n in range(blocks):
-            part = values[:, 8 * n : 8 * n + 8, :].reshape(images * 8, 128)
-            stacked[k * images * 8 : (k + 1) * images * 8, n * 128 : (n + 1) * 128] = part.astype(BF16)
-    patch_cols = col_weight.shape[0]
-    shape = (patch_cols, 3 * images * 8)
+    patch_cols, cols = col_weight.shape
+    shape = (patch_cols, 3 * image_dev * 2 * cols)
     column = lax.broadcasted_iota(jnp.int32, shape, 1)
-    tap_of = column // (images * 8)
-    image_of = (column // 8) % images
+    tap_of = column // (image_dev * 2 * cols)
+    image_of = (column // (2 * cols)) % image_dev
     block_of = (column // cols) % 2
     j_of = column % cols
     across = jnp.zeros(shape, F32)
@@ -160,20 +140,25 @@
     base = jnp.concatenate(lines, axis=0)
     image_of = jnp.concatenate([image_of] * 2, axis=0)
     block_of = jnp.concatenate([block_of] * 2, axis=0)
-    matrix = jnp.concatenate(
-        [
-            jnp.where(jnp.logical_and(image_of == k, block_of == side), base, 0.0)
-            for side in range(2)
-            for k in range(images)
-        ],
-        axis=0,
-    )
-    result = split_dot(matrix, stacked[...]).astype(BF16)
-    rows = target.shape[0]
-    for n in range(blocks):
+    high = base.astype(BF16).astype(F32)
+    patch = base.shape[0]
+    for part, values in enumerate((high, base - high)):
         for side in range(2):
-            at = (2 * n + side) * 128
-            target[:, at : at + 128] = result[side * rows : (side + 1) * rows, n * 128 : (n + 1) * 128]
+            for k in range(image_dev):
+                at = ((part * 2 + side) * image_dev + k) * patch
+                mine = jnp.logical_and(image_of == k, block_of == side)
+                matrix[at : at + patch, :] = jnp.where(mine, values, 0.0).astype(BF16)
+
+
+def select_kernel(dims, dino_list, arrived, chosen, rows_of):
+    slots, per_device, image_dev, capacity = dims
+    rank = lax.axis_index("img")
+    arrived_rows(dino_list, rank, slots, per_device, image_dev, capacity, rows_of)
+    first = arrived.shape[1] - chosen.shape[1]
+    for k in range(chosen.shape[0]):
+        row = rows_of[k]
+        values = arrived[jnp.maximum(row, 0), first:, :]
+        chosen[k] = jnp.where(row >= 0, values, jnp.zeros_like(values))
 
 
 def load_whole(pieces, by_neighbour, whole, sems, first_sem):
@@ -200,32 +185,27 @@
     return jnp.sum(values, axis=-1, keepdims=True)
 
 
-def sam_kernel(
-    counts, dims, sam_list, student, arrived, *rest
-):
+def sam_kernel(counts, dims, sam_list, student, arrived, *rest):
+    sam_pieces, dino_pieces = rest[: counts[0]], rest[counts[0] : sum(counts)]
+    grad, predicted, dino_whole, rows_in, sam_whole, delta, rows_of, sems = rest[sum(counts) :]
+    rows_copy = pltpu.make_async_copy(student, rows_in, sems.at[0])
+    rows_copy.start()
+    sam_copies = load_whole(sam_pieces, True, sam_whole, sems, 1)
+    dino_copies = load_whole(dino_pieces, False, dino_whole, sems, 1 + counts[0])
     slots, per_device, image_dev, capacity = dims
-    sam_pieces, dino_pieces = rest[: counts[0]], rest[counts[0] : sum(counts)]
-    grad, predicted, dino_whole, rows_in, packs_in, sam_whole, delta, row_of, sems = rest[sum(counts) :]
-    rows_copy = pltpu.make_async_copy(student, rows_in, sems.at[0])
-    packs_copy = pltpu.make_async_copy(arrived, packs_in, sems.at[1])
-    rows_copy.start()
-    sam_copies = load_whole(sam_pieces, True, sam_whole, sems, 2)
-    packs_copy.start()
-    dino_copies = load_whole(dino_pieces, False, dino_whole, sems, 2 + counts[0])
     rank = lax.axis_index("img")
-    arrived_rows(sam_list, rank, slots, per_device, image_dev, capacity, row_of)
+    arrived_rows(sam_list, rank, slots, per_device, image_dev, capacity, rows_of)
     for copy in (rows_copy, *sam_copies):
         copy.wait()
     sam_predicted = jnp.dot(rows_in[...], sam_whole[...], preferred_element_type=F32)
-    packs_copy.wait()
     patch = rows_in.shape[0] // image_dev
     for k in range(image_dev):
-        row = row_of[k]
+        row = rows_of[k]
         at = jnp.maximum(row, 0)
         rows = slice(k * patch, (k + 1) * patch)
         for n in range(sam_whole.shape[1] // 128):
             columns = slice(n * 128, (n + 1) * 128)
-            target = packs_in[at, n * patch : (n + 1) * patch, :].astype(F32)
+            target = arrived[at, n * patch : (n + 1) * patch, :].astype(F32)
             error = jnp.clip(sam_predicted[rows, columns] - target, -1.0, 1.0)
             delta[rows, columns] = jnp.where(row >= 0, error, 0.0).astype(BF16)
     grad[...] = lax.dot_general(
@@ -236,7 +216,26 @@
     predicted[...] = jnp.dot(rows_in[...], dino_whole[...], preferred_element_type=F32)
 
 
-def dino_kernel(predicted, target, sam_grad, whole, out, delta):
+def dino_kernel(
+    here, core_side, edge_side, matrix, predicted, sam_grad, whole, out, stacked, target, delta
+):
+    even = lax.rem(lax.axis_index("sp"), 2) == 0
+    images, blocks = here.shape[0], here.shape[1] // 8
+    core = core_side[...].astype(F32)
+    edge = edge_side[...].astype(F32)
+    above = jnp.where(even, edge, core)
+    below = jnp.where(even, core, edge)
+    for k, values in enumerate((above, here[...].astype(F32), below)):
+        for n in range(blocks):
+            part = values[:, 8 * n : 8 * n + 8, :].reshape(images * 8, 128)
+            stacked[k * images * 8 : (k + 1) * images * 8, n * 128 : (n + 1) * 128] = part.astype(BF16)
+    both = jnp.dot(matrix[...], stacked[...], preferred_element_type=F32)
+    rows = predicted.shape[0]
+    both = (both[: 2 * rows] + both[2 * rows :]).astype(BF16)
+    for n in range(blocks):
+        for side in range(2):
+            at = (2 * n + side) * 128
+            target[:, at : at + 128] = both[side * rows : (side + 1) * rows, n * 128 : (n + 1) * 128]
     p = predicted[...]
     t = target[...].astype(F32)
     pred_inv = 1.0 / jnp.sqrt(row_sum(p * p) + EPSILON)
@@ -339,6 +338,15 @@
 
     arrived = lax.all_to_all(packed, "img", split_axis=0, concat_axis=0, tiled=True)
 
+    rows = student.reshape(images * patch, width)
+    matrix = pl.pallas_call(
+        functools.partial(tables_kernel, images),
+        out_shape=jax.ShapeDtypeStruct((4 * images * patch, 6 * images * dino_cols), BF16),
+        in_specs=[SMEM, VMEM, ANY],
+        out_specs=VMEM,
+        compiler_params=params(),
+        name="tables",
+    )(dino_row_weight.T, dino_col_weight, rows)
     if shared:
         chip_perm = [(i, i ^ 2) for i in range(4)]
         near_perm = [(i, i ^ 1) for i in range(peers)]
@@ -351,6 +359,7 @@
         dino_far = [
             lax.ppermute(part, "sp", chip_perm) for part in (dino_shard[:half], dino_shard[half:])
         ]
+        matrix, dino_far[1] = after(matrix, dino_far[1])
         dino_pieces = [dino_proj, core_swap(dino_proj), *dino_far, *map(core_swap, dino_far)]
         sam_pieces = [sam_proj, core_swap(sam_proj), *sam_far, *map(core_swap, sam_far)]
     else:
@@ -367,17 +376,8 @@
         compiler_params=params(),
         name="select",
     )(dino_list, arrived)
-    target = pl.pallas_call(
-        target_kernel,
-        out_shape=jax.ShapeDtypeStruct((images * patch, dino_width), BF16),
-        in_specs=[SMEM] + [VMEM] * 4,
-        out_specs=VMEM,
-        scratch_shapes=[pltpu.VMEM((3 * images * 8, dino_width // 2), BF16)],
-        compiler_params=params(),
-        name="target",
-    )(dino_row_weight.T, dino_col_weight, chosen, core_swap(chosen), edge_swap(chosen))
-
-    rows = student.reshape(images * patch, width)
+    chosen_core, chosen_edge = core_swap(chosen), edge_swap(chosen)
+
     counts = (len(sam_pieces), len(dino_pieces))
     sam_grad, dino_predicted, dino_whole = pl.pallas_call(
         functools.partial(sam_kernel, counts, (slots, *dims)),
@@ -386,15 +386,14 @@
             jax.ShapeDtypeStruct((rows.shape[0], dino_width), F32),
             jax.ShapeDtypeStruct((width, dino_width), BF16),
         ),
-        in_specs=[SMEM] + [ANY] * (2 + sum(counts)),
+        in_specs=[SMEM, ANY, VMEM] + [ANY] * sum(counts),
         out_specs=(VMEM,) * 3,
         scratch_shapes=[
             pltpu.VMEM(rows.shape, BF16),
-            pltpu.VMEM(arrived.shape, BF16),
             pltpu.VMEM((width, sam_width), BF16),
             pltpu.VMEM((rows.shape[0], sam_width), BF16),
             pltpu.SMEM((images,), jnp.int32),
-            pltpu.SemaphoreType.DMA((2 + sum(counts),)),
+            pltpu.SemaphoreType.DMA((1 + sum(counts),)),
         ],
         compiler_params=params(),
         name="sam",
@@ -402,12 +401,16 @@
     out = pl.pallas_call(
         dino_kernel,
         out_shape=jax.ShapeDtypeStruct(rows.shape, BF16),
-        in_specs=[VMEM] * 4,
+        in_specs=[VMEM] * 7,
         out_specs=VMEM,
-        scratch_shapes=[pltpu.VMEM((rows.shape[0], dino_width), BF16)],
+        scratch_shapes=[
+            pltpu.VMEM((6 * images * dino_cols, dino_width // 2), BF16),
+            pltpu.VMEM((rows.shape[0], dino_width), BF16),
+            pltpu.VMEM((rows.shape[0], dino_width), BF16),
+        ],
         compiler_params=params(),
         name="dino",
-    )(dino_predicted, target, sam_grad, dino_whole)
+    )(chosen, chosen_core, chosen_edge, matrix, dino_predicted, sam_grad, dino_whole)
     return out.reshape(student.shape)
 
 

time: 61.8 us -> 59.4 us (0.961)
  starting transfers between devices: 24.4 us -> 23.1 us
  Pallas kernels: 16.7 us -> 15.7 us
  waiting for transfers between devices: 16.3 us -> 17.3 us
  local copies, waits for them, and re-layouts: 3.61 us -> 2.63 us
    ppermute x8, starting transfers between devices: 8.14 us -> 6.86 us  [core_swap(): return lax.ppermute(values, 'sp', core_perm)]
    pallas_call x1, Pallas kernels: 1.92 us -> 0.75 us  [shards(): pl.pallas_call(functools.partial(tables_kernel, images), out_shape=jax.Sh...]
    unnamed x19 -> x17, local copies, waits for them, and re-layouts: 1.77 us -> 0.75 us
    pallas_call x1, Pallas kernels: 2.59 us -> 3.5 us  [shards(): pl.pallas_call(dino_kernel, out_shape=jax.ShapeDtypeStruct(rows.shape, BF...]
    slice x1, local copies, waits for them, and re-layouts: 0.06 us -> 0.84 us  [shards(): dino_shard[:half]]
    dynamic_slice x1, local copies, waits for them, and re-layouts: 1.78 us -> 1.03 us  [shards(): lax.dynamic_slice_in_dim(sam_proj, lax.axis_index('img') % 2 * half, half...]
    ppermute x2, waiting for transfers between devices: 0.96 us -> 1.68 us  [edge_swap(): return lax.ppermute(values, 'sp', edge_perm)]
    pallas_call x1, Pallas kernels: 1.5 us -> 0.84 us  [shards(): pl.pallas_call(functools.partial(select_kernel, (slots, *dims)), out_shap...]
where the time goes in v3:
time: 59.4 us; the launch traced here: 58.9 us
  starting transfers between devices  23.1 us (39%)
  waiting for transfers between devices  17.3 us (29%)
  Pallas kernels  15.7 us (26%)
  local copies, waits for them, and re-layouts  2.63 us (4%)
    ppermute x2, waiting for transfers between devices, shards(): lax.ppermute(part, 'sp', chip_perm)  14.7 us
    ppermute x8, starting transfers between devices, core_swap(): return lax.ppermute(values, 'sp', core_perm)  6.86 us
    ppermute x2, starting transfers between devices, edge_swap(): return lax.ppermute(values, 'sp', edge_perm)  6.4 us
    all_to_all x1, starting transfers between devices, shards(): lax.all_to_all(packed, 'img', split_axis=0, concat_axis=0, tiled=True)  6.13 us
    pallas_call x1, Pallas kernels, shards(): pl.pallas_call(functools.partial(sam_kernel, counts, (slots, *dims)), out...  5.77 us
    pallas_call x1, Pallas kernels, shards(): pl.pallas_call(dino_kernel, out_shape=jax.ShapeDtypeStruct(rows.shape, BF...  3.5 us
    pallas_call x1, Pallas kernels, shards(): pl.pallas_call(functools.partial(pre_kernel, (per_device, grid_rows)), ou...  2.66 us
    ppermute x1, starting transfers between devices, shards(): sam_far.append(lax.ppermute(sam_far[0], 'img', near_perm))  2.24 us
  transfers between devices with their start and end apart: 15, of which 4 were waited for; matrix products, arithmetic and copies ran while one was open for 3% of the time, Pallas kernels for 16%

profile of v3, /device:TPU:1, one launch (start us, length us, event | category | flops | bytes accessed | tf_op | source)
XLA Modules:
  0.0 58.9 jit_solution(17769342971492934160)
XLA Ops:
  0.0 0.0 copy-start.2
  0.0 2.7 %pre.1 = (f32[6,16,1280]{2,1,0:T(8,128)}, bf16[6,8,1280]{2,1,0:T(8,128)(2,1)}, bf16[6,8,1280]{2,1,0:T(8,128)(2,1)}) custom-call(s32[8]{0:T(128)} %start.1, f32[4,8]{1,0:T(4,128)} %bitcast.11, f32[8,16]{1,0:T(8,128)} %col_weight.2, bf16[6,64,1280]{2,1,0:T(8,128)(2,1)} %bitcast.9), custom_call_target="tpu_custom_call" | custom-call | tf_op jit(solution)/shard_map/pre/pallas_call | solution.py:304
  2.7 0.0 collective-permute-start
  2.7 4.5 %collective-permute-start.1 = (bf16[6,8,1280]{2,1,0:T(8,128)(2,1)}, bf16[6,8,1280]{2,1,0:T(8,128)(2,1)S(1)}, u32[]{:S(2)}, u32[]{:S(2)}) collective-permute-start(bf16[6,8,1280]{2,1,0:T(8,128)(2,1)} %get-tuple-element.18), channel_id=1, source_target_pairs={{1,2},{2,1},{5,6},{6,5},{9,10},{10,9},{13,14},{14,13},{17,18},{18,... | collective-permute-start | bytes 368648 | tf_op jit(solution)/shard_map/ppermute | solution.py:298
  7.2 0.0 copy-start.4
  7.3 1.0 %constant_dynamic-slice_fusion = bf16[160,1280]{1,0:T(8,128)(2,1)S(1)} fusion(bf16[320,1280]{1,0:T(8,128)(2,1)} %rest_0_.1, s32[]{:T(128)S(6)} %select_n.11), kind=kLoop, calls=%fused_computation | loop fusion | bytes 819204 | tf_op jit(solution)/shard_map/dynamic_slice | solution.py:354
  8.3 0.0 collective-permute-done.core_part
  8.3 1.7 %collective-permute-done.1.edge_part = bf16[6,8,1280]{2,1,0:T(8,128)(2,1)S(1)} collective-permute-done((bf16[6,8,1280]{2,1,0:T(8,128)(2,1)}, bf16[6,8,1280]{2,1,0:T(8,128)(2,1)S(1)}, u32[]{:S(2)}, u32[]{:S(2)}) %collective-permute-start.1) | collective-permute-done | bytes 122912 | tf_op jit(solution)/shard_map/ppermute | solution.py:298
  10.0 0.6 %copy-done.6 = bf16[6,8,1280]{2,1,0:T(8,128)(2,1)} copy-done((bf16[6,8,1280]{2,1,0:T(8,128)(2,1)}, bf16[6,8,1280]{2,1,0:T(8,128)(2,1)S(1)}, u32[]{:S(2)}) %copy-start.6) | copy-done | bytes 122904
  10.6 2.2 %pack.1 = bf16[16,208,128]{2,1,0:T(8,128)(2,1)} custom-call(s32[48]{0:T(128)} %dino_list.3, s32[48]{0:T(128)} %sam_list.3, bf16[6,4,1536]{2,1,0:T(4,128)(2,1)} %bitcast.10, f32[6,16,1280]{2,1,0:T(8,128)} %get-tuple-element.16.own, bf16[6,8,1280]{2,1,0:T(8,128)(2,1)} %copy-done.5, bf16[6,8,1280]{2,1,0:T(8,128)(2,1)} %copy-done.6), custom_call_target="tpu_custom_call" | custom-call | tf_op jit(solution)/shard_map/pack/pallas_call | solution.py:323
  12.8 6.1 %all-to-all-start = ((bf16[16,208,128]{2,1,0:T(8,128)(2,1)}), bf16[16,208,128]{2,1,0:T(8,128)(2,1)S(1)}, u32[]{:S(2)}, u32[]{:S(2)}) async-start(bf16[16,208,128]{2,1,0:T(8,128)(2,1)} %pack.1), calls=%async_computation | async-start | bytes 1703936 | tf_op jit(solution)/shard_map/all_to_all | solution.py:339
  19.0 1.2 %collective-permute-start.6 = (bf16[320,1280]{1,0:T(8,128)(2,1)}, bf16[320,1280]{1,0:T(8,128)(2,1)}, u32[]{:S(2)}, u32[]{:S(2)}) collective-permute-start(bf16[320,1280]{1,0:T(8,128)(2,1)} %rest_0_.1), channel_id=1, source_target_pairs={{0,1},{1,0},{2,3},{3,2},{4,5},{5,4},{6,7},{7,6},{8,9},{9,8},{10,11... | collective-permute-start | bytes 2457608 | tf_op jit(solution)/shard_map/ppermute | solution.py:295
  20.1 0.1 collective-permute-start.10
  20.2 0.9 %collective-permute-done.4.rest_2_ = bf16[160,1280]{1,0:T(8,128)(2,1)} collective-permute-done((bf16[160,1280]{1,0:T(8,128)(2,1)S(1)}, bf16[160,1280]{1,0:T(8,128)(2,1)}, u32[]{:S(2)}, u32[]{:S(2)}) %collective-permute-start.4) | collective-permute-done | bytes 409632 | tf_op jit(solution)/shard_map/ppermute | solution.py:356
  21.1 0.8 %fusion = (bf16[160,1536]{1,0:T(8,128)(2,1)}, bf16[160,1536]{1,0:T(8,128)(2,1)S(1)}) fusion(bf16[320,1536]{1,0:T(8,128)(2,1)S(1)} %copy-done), kind=kLoop, calls=%fused_computation.1 | loop fusion | bytes 1966080 | tf_op jit(solution)/shard_map/slice | solution.py:360
  21.9 1.5 %collective-permute-start.11 = (bf16[160,1536]{1,0:T(8,128)(2,1)}, bf16[160,1536]{1,0:T(8,128)(2,1)}, u32[]{:S(2)}, u32[]{:S(2)}) collective-permute-start(bf16[160,1536]{1,0:T(8,128)(2,1)} %get-tuple-element.27), channel_id=1, source_target_pairs={{0,2},{1,3},{2,0},{3,1},{4,6},{5,7},{6,4},{7,5},{8,10},{9,11},{10,... | collective-permute-start | bytes 1474568 | tf_op jit(solution)/shard_map/ppermute | solution.py:360
  23.4 2.2 %collective-permute-start.7 = (bf16[160,1280]{1,0:T(8,128)(2,1)}, bf16[160,1280]{1,0:T(8,128)(2,1)}, u32[]{:S(2)}, u32[]{:S(2)}) collective-permute-start(bf16[160,1280]{1,0:T(8,128)(2,1)} %collective-permute-done.4.rest_2_), channel_id=1, source_target_pairs={{0,4},{4,0},{8,12},{12,8},{16,20},{20,16},{24,28},{28,24},{1,5},{5... | collective-permute-start | bytes 1228808 | tf_op jit(solution)/shard_map/ppermute | solution.py:358
  25.6 8.2 %collective-permute-done.5.rest_9_ = bf16[160,1536]{1,0:T(8,128)(2,1)S(1)} collective-permute-done((bf16[160,1536]{1,0:T(8,128)(2,1)S(1)}, bf16[160,1536]{1,0:T(8,128)(2,1)S(1)}, u32[]{:S(2)}, u32[]{:S(2)}) %collective-permute-start.5) | collective-permute-done | bytes 491552 | tf_op jit(solution)/shard_map/ppermute | solution.py:360
  33.8 3.1 %collective-permute-start.8 = (bf16[160,1280]{1,0:T(8,128)(2,1)}, bf16[160,1280]{1,0:T(8,128)(2,1)}, u32[]{:S(2)}, u32[]{:S(2)}) collective-permute-start(bf16[160,1280]{1,0:T(8,128)(2,1)} %collective-permute-done.4.rest_2_), channel_id=1, source_target_pairs={{0,1},{1,0},{2,3},{3,2},{4,5},{5,4},{6,7},{7,6},{8,9},{9,8},{10,11... | collective-permute-start | bytes 1228808 | tf_op jit(solution)/shard_map/ppermute | solution.py:295
  37.0 0.1 copy.13.col_weight
  37.1 0.7 %tables.1.matrix = bf16[768,288]{1,0:T(8,128)(2,1)S(1)} custom-call(f32[3,8]{1,0:T(4,128)S(1)} %bitcast.8, f32[8,4]{1,0:T(8,128)S(1)} %copy.13.col_weight, bf16[192,1280]{1,0:T(8,128)(2,1)S(1)} %bitcast.6), custom_call_target="tpu_custom_call" | custom-call | tf_op jit(solution)/shard_map/tables/pallas_call | solution.py:342
  37.8 0.0 collective-permute-done.6.rest_1_
  37.8 0.1 collective-permute-start.13
  37.9 6.5 %collective-permute-done.11.rest_8_ = bf16[160,1536]{1,0:T(8,128)(2,1)} collective-permute-done((bf16[160,1536]{1,0:T(8,128)(2,1)}, bf16[160,1536]{1,0:T(8,128)(2,1)}, u32[]{:S(2)}, u32[]{:S(2)}) %collective-permute-start.11) | collective-permute-done | bytes 491552 | tf_op jit(solution)/shard_map/ppermute | solution.py:360
  44.4 1.8 %collective-permute-start.12 = (bf16[160,1536]{1,0:T(8,128)(2,1)}, bf16[160,1536]{1,0:T(8,128)(2,1)}, u32[]{:S(2)}, u32[]{:S(2)}) collective-permute-start(bf16[160,1536]{1,0:T(8,128)(2,1)} %collective-permute-done.11.rest_8_), channel_id=1, source_target_pairs={{0,1},{1,0},{2,3},{3,2},{4,5},{5,4},{6,7},{7,6},{8,9},{9,8},{10,11... | collective-permute-start | bytes 1474568 | tf_op jit(solution)/shard_map/ppermute | solution.py:295
  46.2 0.0 collective-permute-start.9
  46.2 0.0 all-to-all-done.arrived
  46.2 0.8 %select.3.here = bf16[12,48,128]{2,1,0:T(8,128)(2,1)S(1)} custom-call(s32[48]{0:T(128)S(1)} %copy-done.2, bf16[16,208,128]{2,1,0:T(8,128)(2,1)S(1)} %all-to-all-done.arrived), custom_call_target="tpu_custom_call" | custom-call | tf_op jit(solution)/shard_map/select/pallas_call | solution.py:370
  47.1 0.6 collective-permute-start.2
  47.6 1.9 %collective-permute-start.3 = (bf16[12,48,128]{2,1,0:T(8,128)(2,1)S(1)}, bf16[12,48,128]{2,1,0:T(8,128)(2,1)S(1)}, u32[]{:S(2)}, u32[]{:S(2)}) collective-permute-start(bf16[12,48,128]{2,1,0:T(8,128)(2,1)S(1)} %select.3.here), channel_id=1, source_target_pairs={{1,2},{2,1},{5,6},{6,5},{9,10},{10,9},{13,14},{14,13},{17,18},{18,... | collective-permute-start | bytes 442376 | tf_op jit(solution)/shard_map/ppermute | solution.py:298
  49.6 5.8 %sam.1 = (bf16[192,1280]{1,0:T(8,128)(2,1)S(1)}, f32[192,1536]{1,0:T(8,128)S(1)}, bf16[1280,1536]{1,0:T(8,128)(2,1)S(1)}) custom-call(s32[48]{0:T(128)S(1)} %copy-done.4, bf16[192,1280]{1,0:T(8,128)(2,1)S(1)} %bitcast.7, bf16[16,208,128]{2,1,0:T(8,128)(2,1)S(1)} %all-to-all-done.arrived, bf16[320,1280]{1,0:T(8,128)(2,1)} %rest_0_.1, ...), custom_call_target="tpu_custom_call" | custom-call | tf_op jit(solution)/shard_map/sam/pallas_call | solution.py:382
  55.4 3.5 %dino.1 = bf16[192,1280]{1,0:T(8,128)(2,1)} custom-call(bf16[12,48,128]{2,1,0:T(8,128)(2,1)S(1)} %select.3.here, bf16[12,48,128]{2,1,0:T(8,128)(2,1)S(1)} %collective-permute-done.2.core_side, bf16[12,48,128]{2,1,0:T(8,128)(2,1)S(1)} %collective-permute-done.3.edge_side, bf16[768,288]{1,0:T(8,128)(2,1)S(1)} %tables.1.matrix, ...), custom_call_target="tpu_custom_call" | custom-call | tf_op jit(solution)/shard_map/dino/pallas_call | solution.py:401
  (23 shorter events, 0.1 us)
Async XLA Ops:
  0.0 20.1 %copy-start = (bf16[320,1536]{1,0:T(8,128)(2,1)S(1)}, bf16[320,1536]{1,0:T(8,128)(2,1)}, u32[]{:S(2)}) copy-start(bf16[320,1536]{1,0:T(8,128)(2,1)} %rest_6_.1) | copy-start | bytes 2949124
  0.0 37.0 %copy-start.7 = (f32[8,4]{0,1:T(4,128)S(1)}, f32[8,4]{0,1:T(4,128)}, u32[]{:S(2)}) copy-start(f32[8,4]{0,1:T(4,128)} %param.20) | copy-start | bytes 388
  0.0 37.0 %copy-start.1 = (bf16[12,2,8,1280]{3,2,1,0:T(8,128)(2,1)S(1)}, bf16[12,2,8,1280]{3,2,1,0:T(8,128)(2,1)}, u32[]{:S(2)}) copy-start(bf16[12,2,8,1280]{3,2,1,0:T(8,128)(2,1)} %param.12) | copy-start | bytes 1474564
  0.0 37.0 %copy-start.3 = (f32[8,3]{0,1:T(4,128)S(1)}, f32[8,3]{0,1:T(4,128)}, u32[]{:S(2)}) copy-start(f32[8,3]{0,1:T(4,128)} %param.19) | copy-start | bytes 292
  0.0 46.2 %copy-start.2 = (s32[48]{0:T(128)S(1)}, s32[48]{0:T(128)}, u32[]{:S(2)}) copy-start(s32[48]{0:T(128)} %dino_list.3) | copy-start | bytes 580
  2.7 5.6 %collective-permute-start = (bf16[6,8,1280]{2,1,0:T(8,128)(2,1)}, bf16[6,8,1280]{2,1,0:T(8,128)(2,1)S(1)}, u32[]{:S(2)}, u32[]{:S(2)}) collective-permute-start(bf16[6,8,1280]{2,1,0:T(8,128)(2,1)} %get-tuple-element.17), channel_id=1, source_target_pairs={{0,1},{1,0},{2,3},{3,2},{4,5},{5,4},{6,7},{7,6},{8,9},{9,8},{10,11... | collective-permute-start | bytes 368648 | tf_op jit(solution)/shard_map/ppermute | solution.py:295
  2.7 7.3 %collective-permute-start.1 = (bf16[6,8,1280]{2,1,0:T(8,128)(2,1)}, bf16[6,8,1280]{2,1,0:T(8,128)(2,1)S(1)}, u32[]{:S(2)}, u32[]{:S(2)}) collective-permute-start(bf16[6,8,1280]{2,1,0:T(8,128)(2,1)} %get-tuple-element.18), channel_id=1, source_target_pairs={{1,2},{2,1},{5,6},{6,5},{9,10},{10,9},{13,14},{14,13},{17,18},{18,... | collective-permute-start | bytes 368648 | tf_op jit(solution)/shard_map/ppermute | solution.py:298
  7.2 42.3 %copy-start.4 = (s32[48]{0:T(128)S(1)}, s32[48]{0:T(128)}, u32[]{:S(2)}) copy-start(s32[48]{0:T(128)} %sam_list.3) | copy-start | bytes 580
  8.3 1.7 %copy-start.5 = (bf16[6,8,1280]{2,1,0:T(8,128)(2,1)}, bf16[6,8,1280]{2,1,0:T(8,128)(2,1)S(1)}, u32[]{:S(2)}) copy-start(bf16[6,8,1280]{2,1,0:T(8,128)(2,1)S(1)} %collective-permute-done.core_part) | copy-start | bytes 368644
  10.0 0.6 %copy-start.6 = (bf16[6,8,1280]{2,1,0:T(8,128)(2,1)}, bf16[6,8,1280]{2,1,0:T(8,128)(2,1)S(1)}, u32[]{:S(2)}) copy-start(bf16[6,8,1280]{2,1,0:T(8,128)(2,1)S(1)} %collective-permute-done.1.edge_part) | copy-start | bytes 368644
  10.0 11.1 %collective-permute-start.4 = (bf16[160,1280]{1,0:T(8,128)(2,1)S(1)}, bf16[160,1280]{1,0:T(8,128)(2,1)}, u32[]{:S(2)}, u32[]{:S(2)}) collective-permute-start(bf16[160,1280]{1,0:T(8,128)(2,1)S(1)} %constant_dynamic-slice_fusion), channel_id=1, source_target_pairs={{0,2},{1,3},{2,0},{3,1},{4,6},{5,7},{6,4},{7,5},{8,10},{9,11},{10,... | collective-permute-start | bytes 1228808 | tf_op jit(solution)/shard_map/ppermute | solution.py:356
  12.8 33.4 %all-to-all-start = ((bf16[16,208,128]{2,1,0:T(8,128)(2,1)}), bf16[16,208,128]{2,1,0:T(8,128)(2,1)S(1)}, u32[]{:S(2)}, u32[]{:S(2)}) async-start(bf16[16,208,128]{2,1,0:T(8,128)(2,1)} %pack.1), calls=%async_computation | async-start | bytes 1703936 | tf_op jit(solution)/shard_map/all_to_all | solution.py:339
  19.0 18.9 %collective-permute-start.6 = (bf16[320,1280]{1,0:T(8,128)(2,1)}, bf16[320,1280]{1,0:T(8,128)(2,1)}, u32[]{:S(2)}, u32[]{:S(2)}) collective-permute-start(bf16[320,1280]{1,0:T(8,128)(2,1)} %rest_0_.1), channel_id=1, source_target_pairs={{0,1},{1,0},{2,3},{3,2},{4,5},{5,4},{6,7},{7,6},{8,9},{9,8},{10,11... | collective-permute-start | bytes 2457608 | tf_op jit(solution)/shard_map/ppermute | solution.py:295
  20.1 27.5 %collective-permute-start.10 = (bf16[320,1536]{1,0:T(8,128)(2,1)S(1)}, bf16[320,1536]{1,0:T(8,128)(2,1)}, u32[]{:S(2)}, u32[]{:S(2)}) collective-permute-start(bf16[320,1536]{1,0:T(8,128)(2,1)S(1)} %copy-done), channel_id=1, source_target_pairs={{0,1},{1,0},{2,3},{3,2},{4,5},{5,4},{6,7},{7,6},{8,9},{9,8},{10,11... | collective-permute-start | bytes 2949128 | tf_op jit(solution)/shard_map/ppermute | solution.py:295
  21.9 11.9 %collective-permute-start.5 = (bf16[160,1536]{1,0:T(8,128)(2,1)S(1)}, bf16[160,1536]{1,0:T(8,128)(2,1)S(1)}, u32[]{:S(2)}, u32[]{:S(2)}) collective-permute-start(bf16[160,1536]{1,0:T(8,128)(2,1)S(1)} %get-tuple-element.28), channel_id=1, source_target_pairs={{0,2},{1,3},{2,0},{3,1},{4,6},{5,7},{6,4},{7,5},{8,10},{9,11},{10,... | collective-permute-start | bytes 1474568 | tf_op jit(solution)/shard_map/ppermute | solution.py:360
  21.9 22.5 %collective-permute-start.11 = (bf16[160,1536]{1,0:T(8,128)(2,1)}, bf16[160,1536]{1,0:T(8,128)(2,1)}, u32[]{:S(2)}, u32[]{:S(2)}) collective-permute-start(bf16[160,1536]{1,0:T(8,128)(2,1)} %get-tuple-element.27), channel_id=1, source_target_pairs={{0,2},{1,3},{2,0},{3,1},{4,6},{5,7},{6,4},{7,5},{8,10},{9,11},{10,... | collective-permute-start | bytes 1474568 | tf_op jit(solution)/shard_map/ppermute | solution.py:360
  23.4 22.8 %collective-permute-start.7 = (bf16[160,1280]{1,0:T(8,128)(2,1)}, bf16[160,1280]{1,0:T(8,128)(2,1)}, u32[]{:S(2)}, u32[]{:S(2)}) collective-permute-start(bf16[160,1280]{1,0:T(8,128)(2,1)} %collective-permute-done.4.rest_2_), channel_id=1, source_target_pairs={{0,4},{4,0},{8,12},{12,8},{16,20},{20,16},{24,28},{28,24},{1,5},{5... | collective-permute-start | bytes 1228808 | tf_op jit(solution)/shard_map/ppermute | solution.py:358
  33.8 13.2 %collective-permute-start.8 = (bf16[160,1280]{1,0:T(8,128)(2,1)}, bf16[160,1280]{1,0:T(8,128)(2,1)}, u32[]{:S(2)}, u32[]{:S(2)}) collective-permute-start(bf16[160,1280]{1,0:T(8,128)(2,1)} %collective-permute-done.4.rest_2_), channel_id=1, source_target_pairs={{0,1},{1,0},{2,3},{3,2},{4,5},{5,4},{6,7},{7,6},{8,9},{9,8},{10,11... | collective-permute-start | bytes 1228808 | tf_op jit(solution)/shard_map/ppermute | solution.py:295
  37.8 11.8 %collective-permute-start.13 = (bf16[160,1536]{1,0:T(8,128)(2,1)S(1)}, bf16[160,1536]{1,0:T(8,128)(2,1)}, u32[]{:S(2)}, u32[]{:S(2)}) collective-permute-start(bf16[160,1536]{1,0:T(8,128)(2,1)S(1)} %collective-permute-done.5.rest_9_), channel_id=1, source_target_pairs={{0,1},{1,0},{2,3},{3,2},{4,5},{5,4},{6,7},{7,6},{8,9},{9,8},{10,11... | collective-permute-start | bytes 1474568 | tf_op jit(solution)/shard_map/ppermute | solution.py:295
  44.4 5.2 %collective-permute-start.12 = (bf16[160,1536]{1,0:T(8,128)(2,1)}, bf16[160,1536]{1,0:T(8,128)(2,1)}, u32[]{:S(2)}, u32[]{:S(2)}) collective-permute-start(bf16[160,1536]{1,0:T(8,128)(2,1)} %collective-permute-done.11.rest_8_), channel_id=1, source_target_pairs={{0,1},{1,0},{2,3},{3,2},{4,5},{5,4},{6,7},{7,6},{8,9},{9,8},{10,11... | collective-permute-start | bytes 1474568 | tf_op jit(solution)/shard_map/ppermute | solution.py:295
  46.2 3.4 %collective-permute-start.9 = (bf16[160,1280]{1,0:T(8,128)(2,1)}, bf16[160,1280]{1,0:T(8,128)(2,1)}, u32[]{:S(2)}, u32[]{:S(2)}) collective-permute-start(bf16[160,1280]{1,0:T(8,128)(2,1)} %collective-permute-done.7.rest_3_), channel_id=1, source_target_pairs={{0,1},{1,0},{2,3},{3,2},{4,5},{5,4},{6,7},{7,6},{8,9},{9,8},{10,11... | collective-permute-start | bytes 1228808 | tf_op jit(solution)/shard_map/ppermute | solution.py:295
  47.1 8.3 %collective-permute-start.2 = (bf16[12,48,128]{2,1,0:T(8,128)(2,1)S(1)}, bf16[12,48,128]{2,1,0:T(8,128)(2,1)S(1)}, u32[]{:S(2)}, u32[]{:S(2)}) collective-permute-start(bf16[12,48,128]{2,1,0:T(8,128)(2,1)S(1)} %select.3.here), channel_id=1, source_target_pairs={{0,1},{1,0},{2,3},{3,2},{4,5},{5,4},{6,7},{7,6},{8,9},{9,8},{10,11... | collective-permute-start | bytes 442376 | tf_op jit(solution)/shard_map/ppermute | solution.py:295
  47.6 7.8 %collective-permute-start.3 = (bf16[12,48,128]{2,1,0:T(8,128)(2,1)S(1)}, bf16[12,48,128]{2,1,0:T(8,128)(2,1)S(1)}, u32[]{:S(2)}, u32[]{:S(2)}) collective-permute-start(bf16[12,48,128]{2,1,0:T(8,128)(2,1)S(1)} %select.3.here), channel_id=1, source_target_pairs={{1,2},{2,1},{5,6},{6,5},{9,10},{10,9},{13,14},{14,13},{17,18},{18,... | collective-permute-start | bytes 442376 | tf_op jit(solution)/shard_map/ppermute | solution.py:298

commit v4 on v3

--- a/solution.py
+++ b/solution.py
@@ -48,12 +48,12 @@
 
     def source(peer, _):
         def slot(i, seen):
-            image = list_ref[peer * per_device + i]
-            mine = lax.div(image, image_dev) == rank
+            local = list_ref[peer * per_device + i] - rank * image_dev
+            mine = jnp.logical_and(local >= 0, local < image_dev)
 
             @pl.when(mine)
             def _():
-                row_of[image - rank * image_dev] = peer * capacity + seen
+                row_of[local] = peer * capacity + seen
 
             return seen + jnp.where(mine, 1, 0)
 

time: 59.4 us -> 59.3 us (level)
  no operation moved by 1% of the time
where the time goes in v4:
time: 59.3 us; the launch traced here: 58.8 us
  starting transfers between devices  23.1 us (39%)
  waiting for transfers between devices  17.3 us (29%)
  Pallas kernels  15.6 us (26%)
  local copies, waits for them, and re-layouts  2.63 us (4%)
    ppermute x2, waiting for transfers between devices, shards(): lax.ppermute(part, 'sp', chip_perm)  14.7 us
    ppermute x8, starting transfers between devices, core_swap(): return lax.ppermute(values, 'sp', core_perm)  6.86 us
    ppermute x2, starting transfers between devices, edge_swap(): return lax.ppermute(values, 'sp', edge_perm)  6.4 us
    all_to_all x1, starting transfers between devices, shards(): lax.all_to_all(packed, 'img', split_axis=0, concat_axis=0, tiled=True)  6.13 us
    pallas_call x1, Pallas kernels, shards(): pl.pallas_call(functools.partial(sam_kernel, counts, (slots, *dims)), out...  5.78 us
    pallas_call x1, Pallas kernels, shards(): pl.pallas_call(dino_kernel, out_shape=jax.ShapeDtypeStruct(rows.shape, BF...  3.5 us
    pallas_call x1, Pallas kernels, shards(): pl.pallas_call(functools.partial(pre_kernel, (per_device, grid_rows)), ou...  2.66 us
    ppermute x1, starting transfers between devices, shards(): sam_far.append(lax.ppermute(sam_far[0], 'img', near_perm))  2.24 us
  transfers between devices with their start and end apart: 15, of which 4 were waited for; matrix products, arithmetic and copies ran while one was open for 3% of the time, Pallas kernels for 16%

profile of v4, /device:TPU:1, one launch (start us, length us, event | category | flops | bytes accessed | tf_op | source)
XLA Modules:
  0.0 58.8 jit_solution(4809806053735807762)
XLA Ops:
  0.0 0.0 copy-start.2
  0.0 2.7 %pre.1 = (f32[6,16,1280]{2,1,0:T(8,128)}, bf16[6,8,1280]{2,1,0:T(8,128)(2,1)}, bf16[6,8,1280]{2,1,0:T(8,128)(2,1)}) custom-call(s32[8]{0:T(128)} %start.1, f32[4,8]{1,0:T(4,128)} %bitcast.11, f32[8,16]{1,0:T(8,128)} %col_weight.2, bf16[6,64,1280]{2,1,0:T(8,128)(2,1)} %bitcast.9), custom_call_target="tpu_custom_call" | custom-call | tf_op jit(solution)/shard_map/pre/pallas_call | solution.py:304
  2.7 0.0 collective-permute-start
  2.7 4.5 %collective-permute-start.1 = (bf16[6,8,1280]{2,1,0:T(8,128)(2,1)}, bf16[6,8,1280]{2,1,0:T(8,128)(2,1)S(1)}, u32[]{:S(2)}, u32[]{:S(2)}) collective-permute-start(bf16[6,8,1280]{2,1,0:T(8,128)(2,1)} %get-tuple-element.18), channel_id=1, source_target_pairs={{1,2},{2,1},{5,6},{6,5},{9,10},{10,9},{13,14},{14,13},{17,18},{18,... | collective-permute-start | bytes 368648 | tf_op jit(solution)/shard_map/ppermute | solution.py:298
  7.2 0.0 copy-start.4
  7.3 1.0 %constant_dynamic-slice_fusion = bf16[160,1280]{1,0:T(8,128)(2,1)S(1)} fusion(bf16[320,1280]{1,0:T(8,128)(2,1)} %rest_0_.1, s32[]{:T(128)S(6)} %select_n.11), kind=kLoop, calls=%fused_computation | loop fusion | bytes 819204 | tf_op jit(solution)/shard_map/dynamic_slice | solution.py:354
  8.3 0.0 collective-permute-done.core_part
  8.3 1.7 %collective-permute-done.1.edge_part = bf16[6,8,1280]{2,1,0:T(8,128)(2,1)S(1)} collective-permute-done((bf16[6,8,1280]{2,1,0:T(8,128)(2,1)}, bf16[6,8,1280]{2,1,0:T(8,128)(2,1)S(1)}, u32[]{:S(2)}, u32[]{:S(2)}) %collective-permute-start.1) | collective-permute-done | bytes 122912 | tf_op jit(solution)/shard_map/ppermute | solution.py:298
  10.0 0.0 collective-permute-start.4
  10.0 0.6 %copy-done.6 = bf16[6,8,1280]{2,1,0:T(8,128)(2,1)} copy-done((bf16[6,8,1280]{2,1,0:T(8,128)(2,1)}, bf16[6,8,1280]{2,1,0:T(8,128)(2,1)S(1)}, u32[]{:S(2)}) %copy-start.6) | copy-done | bytes 122904
  10.6 2.2 %pack.1 = bf16[16,208,128]{2,1,0:T(8,128)(2,1)} custom-call(s32[48]{0:T(128)} %dino_list.3, s32[48]{0:T(128)} %sam_list.3, bf16[6,4,1536]{2,1,0:T(4,128)(2,1)} %bitcast.10, f32[6,16,1280]{2,1,0:T(8,128)} %get-tuple-element.16.own, bf16[6,8,1280]{2,1,0:T(8,128)(2,1)} %copy-done.5, bf16[6,8,1280]{2,1,0:T(8,128)(2,1)} %copy-done.6), custom_call_target="tpu_custom_call" | custom-call | tf_op jit(solution)/shard_map/pack/pallas_call | solution.py:323
  12.8 6.1 %all-to-all-start = ((bf16[16,208,128]{2,1,0:T(8,128)(2,1)}), bf16[16,208,128]{2,1,0:T(8,128)(2,1)S(1)}, u32[]{:S(2)}, u32[]{:S(2)}) async-start(bf16[16,208,128]{2,1,0:T(8,128)(2,1)} %pack.1), calls=%async_computation | async-start | bytes 1703936 | tf_op jit(solution)/shard_map/all_to_all | solution.py:339
  19.0 1.2 %collective-permute-start.6 = (bf16[320,1280]{1,0:T(8,128)(2,1)}, bf16[320,1280]{1,0:T(8,128)(2,1)}, u32[]{:S(2)}, u32[]{:S(2)}) collective-permute-start(bf16[320,1280]{1,0:T(8,128)(2,1)} %rest_0_.1), channel_id=1, source_target_pairs={{0,1},{1,0},{2,3},{3,2},{4,5},{5,4},{6,7},{7,6},{8,9},{9,8},{10,11... | collective-permute-start | bytes 2457608 | tf_op jit(solution)/shard_map/ppermute | solution.py:295
  20.1 0.1 collective-permute-start.10
  20.2 0.9 %collective-permute-done.4.rest_2_ = bf16[160,1280]{1,0:T(8,128)(2,1)} collective-permute-done((bf16[160,1280]{1,0:T(8,128)(2,1)S(1)}, bf16[160,1280]{1,0:T(8,128)(2,1)}, u32[]{:S(2)}, u32[]{:S(2)}) %collective-permute-start.4) | collective-permute-done | bytes 409632 | tf_op jit(solution)/shard_map/ppermute | solution.py:356
  21.1 0.8 %fusion = (bf16[160,1536]{1,0:T(8,128)(2,1)}, bf16[160,1536]{1,0:T(8,128)(2,1)S(1)}) fusion(bf16[320,1536]{1,0:T(8,128)(2,1)S(1)} %copy-done), kind=kLoop, calls=%fused_computation.1 | loop fusion | bytes 1966080 | tf_op jit(solution)/shard_map/slice | solution.py:360
  21.9 0.0 collective-permute-start.5
  21.9 1.5 %collective-permute-start.11 = (bf16[160,1536]{1,0:T(8,128)(2,1)}, bf16[160,1536]{1,0:T(8,128)(2,1)}, u32[]{:S(2)}, u32[]{:S(2)}) collective-permute-start(bf16[160,1536]{1,0:T(8,128)(2,1)} %get-tuple-element.27), channel_id=1, source_target_pairs={{0,2},{1,3},{2,0},{3,1},{4,6},{5,7},{6,4},{7,5},{8,10},{9,11},{10,... | collective-permute-start | bytes 1474568 | tf_op jit(solution)/shard_map/ppermute | solution.py:360
  23.4 2.2 %collective-permute-start.7 = (bf16[160,1280]{1,0:T(8,128)(2,1)}, bf16[160,1280]{1,0:T(8,128)(2,1)}, u32[]{:S(2)}, u32[]{:S(2)}) collective-permute-start(bf16[160,1280]{1,0:T(8,128)(2,1)} %collective-permute-done.4.rest_2_), channel_id=1, source_target_pairs={{0,4},{4,0},{8,12},{12,8},{16,20},{20,16},{24,28},{28,24},{1,5},{5... | collective-permute-start | bytes 1228808 | tf_op jit(solution)/shard_map/ppermute | solution.py:358
  25.6 8.2 %collective-permute-done.5.rest_9_ = bf16[160,1536]{1,0:T(8,128)(2,1)S(1)} collective-permute-done((bf16[160,1536]{1,0:T(8,128)(2,1)S(1)}, bf16[160,1536]{1,0:T(8,128)(2,1)S(1)}, u32[]{:S(2)}, u32[]{:S(2)}) %collective-permute-start.5) | collective-permute-done | bytes 491552 | tf_op jit(solution)/shard_map/ppermute | solution.py:360
  33.8 3.1 %collective-permute-start.8 = (bf16[160,1280]{1,0:T(8,128)(2,1)}, bf16[160,1280]{1,0:T(8,128)(2,1)}, u32[]{:S(2)}, u32[]{:S(2)}) collective-permute-start(bf16[160,1280]{1,0:T(8,128)(2,1)} %collective-permute-done.4.rest_2_), channel_id=1, source_target_pairs={{0,1},{1,0},{2,3},{3,2},{4,5},{5,4},{6,7},{7,6},{8,9},{9,8},{10,11... | collective-permute-start | bytes 1228808 | tf_op jit(solution)/shard_map/ppermute | solution.py:295
  37.0 0.1 copy.13.col_weight
  37.1 0.7 %tables.1.matrix = bf16[768,288]{1,0:T(8,128)(2,1)S(1)} custom-call(f32[3,8]{1,0:T(4,128)S(1)} %bitcast.8, f32[8,4]{1,0:T(8,128)S(1)} %copy.13.col_weight, bf16[192,1280]{1,0:T(8,128)(2,1)S(1)} %bitcast.6), custom_call_target="tpu_custom_call" | custom-call | tf_op jit(solution)/shard_map/tables/pallas_call | solution.py:342
  37.8 0.1 collective-permute-start.13
  37.9 6.5 %collective-permute-done.11.rest_8_ = bf16[160,1536]{1,0:T(8,128)(2,1)} collective-permute-done((bf16[160,1536]{1,0:T(8,128)(2,1)}, bf16[160,1536]{1,0:T(8,128)(2,1)}, u32[]{:S(2)}, u32[]{:S(2)}) %collective-permute-start.11) | collective-permute-done | bytes 491552 | tf_op jit(solution)/shard_map/ppermute | solution.py:360
  44.4 1.8 %collective-permute-start.12 = (bf16[160,1536]{1,0:T(8,128)(2,1)}, bf16[160,1536]{1,0:T(8,128)(2,1)}, u32[]{:S(2)}, u32[]{:S(2)}) collective-permute-start(bf16[160,1536]{1,0:T(8,128)(2,1)} %collective-permute-done.11.rest_8_), channel_id=1, source_target_pairs={{0,1},{1,0},{2,3},{3,2},{4,5},{5,4},{6,7},{7,6},{8,9},{9,8},{10,11... | collective-permute-start | bytes 1474568 | tf_op jit(solution)/shard_map/ppermute | solution.py:295
  46.2 0.0 collective-permute-start.9
  46.2 0.8 %select.3.here = bf16[12,48,128]{2,1,0:T(8,128)(2,1)S(1)} custom-call(s32[48]{0:T(128)S(1)} %copy-done.2, bf16[16,208,128]{2,1,0:T(8,128)(2,1)S(1)} %all-to-all-done.arrived), custom_call_target="tpu_custom_call" | custom-call | tf_op jit(solution)/shard_map/select/pallas_call | solution.py:370
  47.0 0.6 collective-permute-start.2
  47.6 1.9 %collective-permute-start.3 = (bf16[12,48,128]{2,1,0:T(8,128)(2,1)S(1)}, bf16[12,48,128]{2,1,0:T(8,128)(2,1)S(1)}, u32[]{:S(2)}, u32[]{:S(2)}) collective-permute-start(bf16[12,48,128]{2,1,0:T(8,128)(2,1)S(1)} %select.3.here), channel_id=1, source_target_pairs={{1,2},{2,1},{5,6},{6,5},{9,10},{10,9},{13,14},{14,13},{17,18},{18,... | collective-permute-start | bytes 442376 | tf_op jit(solution)/shard_map/ppermute | solution.py:298
  49.5 5.8 %sam.1 = (bf16[192,1280]{1,0:T(8,128)(2,1)S(1)}, f32[192,1536]{1,0:T(8,128)S(1)}, bf16[1280,1536]{1,0:T(8,128)(2,1)S(1)}) custom-call(s32[48]{0:T(128)S(1)} %copy-done.4, bf16[192,1280]{1,0:T(8,128)(2,1)S(1)} %bitcast.7, bf16[16,208,128]{2,1,0:T(8,128)(2,1)S(1)} %all-to-all-done.arrived, bf16[320,1280]{1,0:T(8,128)(2,1)} %rest_0_.1, ...), custom_call_target="tpu_custom_call" | custom-call | tf_op jit(solution)/shard_map/sam/pallas_call | solution.py:382
  55.3 3.5 %dino.1 = bf16[192,1280]{1,0:T(8,128)(2,1)} custom-call(bf16[12,48,128]{2,1,0:T(8,128)(2,1)S(1)} %select.3.here, bf16[12,48,128]{2,1,0:T(8,128)(2,1)S(1)} %collective-permute-done.2.core_side, bf16[12,48,128]{2,1,0:T(8,128)(2,1)S(1)} %collective-permute-done.3.edge_side, bf16[768,288]{1,0:T(8,128)(2,1)S(1)} %tables.1.matrix, ...), custom_call_target="tpu_custom_call" | custom-call | tf_op jit(solution)/shard_map/dino/pallas_call | solution.py:401
  (23 shorter events, 0.1 us)
Async XLA Ops:
  0.0 20.1 %copy-start = (bf16[320,1536]{1,0:T(8,128)(2,1)S(1)}, bf16[320,1536]{1,0:T(8,128)(2,1)}, u32[]{:S(2)}) copy-start(bf16[320,1536]{1,0:T(8,128)(2,1)} %rest_6_.1) | copy-start | bytes 2949124
  0.0 37.0 %copy-start.7 = (f32[8,4]{0,1:T(4,128)S(1)}, f32[8,4]{0,1:T(4,128)}, u32[]{:S(2)}) copy-start(f32[8,4]{0,1:T(4,128)} %param.20) | copy-start | bytes 388
  0.0 37.0 %copy-start.1 = (bf16[12,2,8,1280]{3,2,1,0:T(8,128)(2,1)S(1)}, bf16[12,2,8,1280]{3,2,1,0:T(8,128)(2,1)}, u32[]{:S(2)}) copy-start(bf16[12,2,8,1280]{3,2,1,0:T(8,128)(2,1)} %param.12) | copy-start | bytes 1474564
  0.0 37.0 %copy-start.3 = (f32[8,3]{0,1:T(4,128)S(1)}, f32[8,3]{0,1:T(4,128)}, u32[]{:S(2)}) copy-start(f32[8,3]{0,1:T(4,128)} %param.19) | copy-start | bytes 292
  0.0 46.2 %copy-start.2 = (s32[48]{0:T(128)S(1)}, s32[48]{0:T(128)}, u32[]{:S(2)}) copy-start(s32[48]{0:T(128)} %dino_list.3) | copy-start | bytes 580
  2.7 5.6 %collective-permute-start = (bf16[6,8,1280]{2,1,0:T(8,128)(2,1)}, bf16[6,8,1280]{2,1,0:T(8,128)(2,1)S(1)}, u32[]{:S(2)}, u32[]{:S(2)}) collective-permute-start(bf16[6,8,1280]{2,1,0:T(8,128)(2,1)} %get-tuple-element.17), channel_id=1, source_target_pairs={{0,1},{1,0},{2,3},{3,2},{4,5},{5,4},{6,7},{7,6},{8,9},{9,8},{10,11... | collective-permute-start | bytes 368648 | tf_op jit(solution)/shard_map/ppermute | solution.py:295
  2.7 7.3 %collective-permute-start.1 = (bf16[6,8,1280]{2,1,0:T(8,128)(2,1)}, bf16[6,8,1280]{2,1,0:T(8,128)(2,1)S(1)}, u32[]{:S(2)}, u32[]{:S(2)}) collective-permute-start(bf16[6,8,1280]{2,1,0:T(8,128)(2,1)} %get-tuple-element.18), channel_id=1, source_target_pairs={{1,2},{2,1},{5,6},{6,5},{9,10},{10,9},{13,14},{14,13},{17,18},{18,... | collective-permute-start | bytes 368648 | tf_op jit(solution)/shard_map/ppermute | solution.py:298
  7.2 42.3 %copy-start.4 = (s32[48]{0:T(128)S(1)}, s32[48]{0:T(128)}, u32[]{:S(2)}) copy-start(s32[48]{0:T(128)} %sam_list.3) | copy-start | bytes 580
  8.3 1.7 %copy-start.5 = (bf16[6,8,1280]{2,1,0:T(8,128)(2,1)}, bf16[6,8,1280]{2,1,0:T(8,128)(2,1)S(1)}, u32[]{:S(2)}) copy-start(bf16[6,8,1280]{2,1,0:T(8,128)(2,1)S(1)} %collective-permute-done.core_part) | copy-start | bytes 368644
  10.0 0.6 %copy-start.6 = (bf16[6,8,1280]{2,1,0:T(8,128)(2,1)}, bf16[6,8,1280]{2,1,0:T(8,128)(2,1)S(1)}, u32[]{:S(2)}) copy-start(bf16[6,8,1280]{2,1,0:T(8,128)(2,1)S(1)} %collective-permute-done.1.edge_part) | copy-start | bytes 368644
  10.0 11.1 %collective-permute-start.4 = (bf16[160,1280]{1,0:T(8,128)(2,1)S(1)}, bf16[160,1280]{1,0:T(8,128)(2,1)}, u32[]{:S(2)}, u32[]{:S(2)}) collective-permute-start(bf16[160,1280]{1,0:T(8,128)(2,1)S(1)} %constant_dynamic-slice_fusion), channel_id=1, source_target_pairs={{0,2},{1,3},{2,0},{3,1},{4,6},{5,7},{6,4},{7,5},{8,10},{9,11},{10,... | collective-permute-start | bytes 1228808 | tf_op jit(solution)/shard_map/ppermute | solution.py:356
  12.8 33.4 %all-to-all-start = ((bf16[16,208,128]{2,1,0:T(8,128)(2,1)}), bf16[16,208,128]{2,1,0:T(8,128)(2,1)S(1)}, u32[]{:S(2)}, u32[]{:S(2)}) async-start(bf16[16,208,128]{2,1,0:T(8,128)(2,1)} %pack.1), calls=%async_computation | async-start | bytes 1703936 | tf_op jit(solution)/shard_map/all_to_all | solution.py:339
  19.0 18.9 %collective-permute-start.6 = (bf16[320,1280]{1,0:T(8,128)(2,1)}, bf16[320,1280]{1,0:T(8,128)(2,1)}, u32[]{:S(2)}, u32[]{:S(2)}) collective-permute-start(bf16[320,1280]{1,0:T(8,128)(2,1)} %rest_0_.1), channel_id=1, source_target_pairs={{0,1},{1,0},{2,3},{3,2},{4,5},{5,4},{6,7},{7,6},{8,9},{9,8},{10,11... | collective-permute-start | bytes 2457608 | tf_op jit(solution)/shard_map/ppermute | solution.py:295
  20.1 27.5 %collective-permute-start.10 = (bf16[320,1536]{1,0:T(8,128)(2,1)S(1)}, bf16[320,1536]{1,0:T(8,128)(2,1)}, u32[]{:S(2)}, u32[]{:S(2)}) collective-permute-start(bf16[320,1536]{1,0:T(8,128)(2,1)S(1)} %copy-done), channel_id=1, source_target_pairs={{0,1},{1,0},{2,3},{3,2},{4,5},{5,4},{6,7},{7,6},{8,9},{9,8},{10,11... | collective-permute-start | bytes 2949128 | tf_op jit(solution)/shard_map/ppermute | solution.py:295
  21.9 11.9 %collective-permute-start.5 = (bf16[160,1536]{1,0:T(8,128)(2,1)S(1)}, bf16[160,1536]{1,0:T(8,128)(2,1)S(1)}, u32[]{:S(2)}, u32[]{:S(2)}) collective-permute-start(bf16[160,1536]{1,0:T(8,128)(2,1)S(1)} %get-tuple-element.28), channel_id=1, source_target_pairs={{0,2},{1,3},{2,0},{3,1},{4,6},{5,7},{6,4},{7,5},{8,10},{9,11},{10,... | collective-permute-start | bytes 1474568 | tf_op jit(solution)/shard_map/ppermute | solution.py:360
  21.9 22.5 %collective-permute-start.11 = (bf16[160,1536]{1,0:T(8,128)(2,1)}, bf16[160,1536]{1,0:T(8,128)(2,1)}, u32[]{:S(2)}, u32[]{:S(2)}) collective-permute-start(bf16[160,1536]{1,0:T(8,128)(2,1)} %get-tuple-element.27), channel_id=1, source_target_pairs={{0,2},{1,3},{2,0},{3,1},{4,6},{5,7},{6,4},{7,5},{8,10},{9,11},{10,... | collective-permute-start | bytes 1474568 | tf_op jit(solution)/shard_map/ppermute | solution.py:360
  23.4 22.8 %collective-permute-start.7 = (bf16[160,1280]{1,0:T(8,128)(2,1)}, bf16[160,1280]{1,0:T(8,128)(2,1)}, u32[]{:S(2)}, u32[]{:S(2)}) collective-permute-start(bf16[160,1280]{1,0:T(8,128)(2,1)} %collective-permute-done.4.rest_2_), channel_id=1, source_target_pairs={{0,4},{4,0},{8,12},{12,8},{16,20},{20,16},{24,28},{28,24},{1,5},{5... | collective-permute-start | bytes 1228808 | tf_op jit(solution)/shard_map/ppermute | solution.py:358
  33.8 13.2 %collective-permute-start.8 = (bf16[160,1280]{1,0:T(8,128)(2,1)}, bf16[160,1280]{1,0:T(8,128)(2,1)}, u32[]{:S(2)}, u32[]{:S(2)}) collective-permute-start(bf16[160,1280]{1,0:T(8,128)(2,1)} %collective-permute-done.4.rest_2_), channel_id=1, source_target_pairs={{0,1},{1,0},{2,3},{3,2},{4,5},{5,4},{6,7},{7,6},{8,9},{9,8},{10,11... | collective-permute-start | bytes 1228808 | tf_op jit(solution)/shard_map/ppermute | solution.py:295
  37.8 11.7 %collective-permute-start.13 = (bf16[160,1536]{1,0:T(8,128)(2,1)S(1)}, bf16[160,1536]{1,0:T(8,128)(2,1)}, u32[]{:S(2)}, u32[]{:S(2)}) collective-permute-start(bf16[160,1536]{1,0:T(8,128)(2,1)S(1)} %collective-permute-done.5.rest_9_), channel_id=1, source_target_pairs={{0,1},{1,0},{2,3},{3,2},{4,5},{5,4},{6,7},{7,6},{8,9},{9,8},{10,11... | collective-permute-start | bytes 1474568 | tf_op jit(solution)/shard_map/ppermute | solution.py:295
  44.4 5.1 %collective-permute-start.12 = (bf16[160,1536]{1,0:T(8,128)(2,1)}, bf16[160,1536]{1,0:T(8,128)(2,1)}, u32[]{:S(2)}, u32[]{:S(2)}) collective-permute-start(bf16[160,1536]{1,0:T(8,128)(2,1)} %collective-permute-done.11.rest_8_), channel_id=1, source_target_pairs={{0,1},{1,0},{2,3},{3,2},{4,5},{5,4},{6,7},{7,6},{8,9},{9,8},{10,11... | collective-permute-start | bytes 1474568 | tf_op jit(solution)/shard_map/ppermute | solution.py:295
  46.2 3.3 %collective-permute-start.9 = (bf16[160,1280]{1,0:T(8,128)(2,1)}, bf16[160,1280]{1,0:T(8,128)(2,1)}, u32[]{:S(2)}, u32[]{:S(2)}) collective-permute-start(bf16[160,1280]{1,0:T(8,128)(2,1)} %collective-permute-done.7.rest_3_), channel_id=1, source_target_pairs={{0,1},{1,0},{2,3},{3,2},{4,5},{5,4},{6,7},{7,6},{8,9},{9,8},{10,11... | collective-permute-start | bytes 1228808 | tf_op jit(solution)/shard_map/ppermute | solution.py:295
  47.0 8.3 %collective-permute-start.2 = (bf16[12,48,128]{2,1,0:T(8,128)(2,1)S(1)}, bf16[12,48,128]{2,1,0:T(8,128)(2,1)S(1)}, u32[]{:S(2)}, u32[]{:S(2)}) collective-permute-start(bf16[12,48,128]{2,1,0:T(8,128)(2,1)S(1)} %select.3.here), channel_id=1, source_target_pairs={{0,1},{1,0},{2,3},{3,2},{4,5},{5,4},{6,7},{7,6},{8,9},{9,8},{10,11... | collective-permute-start | bytes 442376 | tf_op jit(solution)/shard_map/ppermute | solution.py:295
  47.6 7.8 %collective-permute-start.3 = (bf16[12,48,128]{2,1,0:T(8,128)(2,1)S(1)}, bf16[12,48,128]{2,1,0:T(8,128)(2,1)S(1)}, u32[]{:S(2)}, u32[]{:S(2)}) collective-permute-start(bf16[12,48,128]{2,1,0:T(8,128)(2,1)S(1)} %select.3.here), channel_id=1, source_target_pairs={{1,2},{2,1},{5,6},{6,5},{9,10},{10,9},{13,14},{14,13},{17,18},{18,... | collective-permute-start | bytes 442376 | tf_op jit(solution)/shard_map/ppermute | solution.py:298
